TPU v7x, 256 devices: a whole 4x4x8 slice. The times are simulated.
256 devices in a mesh: band: 4 (over z_hi), fft: 64 (over x, z_lo, y, core).
Axes of the slice: x: 4, y: 4, z: 8 (z_hi: 4, z_lo: 2; z = z_hi * 2 + z_lo), core: 2. Of those that a mesh axis runs over, the one named last changes fastest.
Arguments:
- wave_coef: float32 [2, 8, 160, 8192], P(None, 'band', None, 'fft'), may hold values from -6 to 6
- stick_map: int32 [8192], P('fft'), may hold values from 0 to 25599, as said below
- local_potential: float32 [192, 25600], P('fft'), may hold values from -6 to 6
- core_density: float32 [192, 25600], P('fft'), may hold values from 0.05 to 1
- occupations: float32 [8], P('band'), may hold values from 0.5 to 2
- block_place: int32 [6144], P('fft'), may hold values from 0 to 599, as said below
- block_atom: int32 [6144], P('fft'), may hold values from 0 to 1023, as said below
- projectors: float32 [6144, 64, 128], P('fft'), may hold values from -0.5 to 0.5
- coupling: float32 [64, 64], replicated, may hold values from -0.75 to 0.75
Outputs:
- applied: float32 [2, 8, 160, 8192], P(None, 'band', None, 'fft')
- density: float32 [192, 25600], P('fft')
- exchange_field: float32 [192, 25600], P('fft')
Inputs may be any that keep to these rules, and one draw needn't show every extreme that they name: `stick_map`: values are distinct; the 8192 sticks are the columns of smallest (x / 160)^2 + (y / 160)^2 in signed frequencies, ties in any order, placed along the array in any order. `block_place`: on fft index f the 96 entries never fall, lie in blocks of the slots s with s * 64 + f < 160, and the last is the last block of those slots. `block_atom`: on fft index f every entry is (f * 16 - 16 // 2 + i) mod 1024 for some i < 32, and each such atom appears there.
All inputs are finite; a program needn't handle non-finite values.
Results may differ from a plain program's by a relative error of at most 0.0001.
Values sent between devices are 32-bit elements; how exact they have to be, the bound alone decides.
A program may use at most 192 MiB of HBM per device.

v0:
```python
import math

import jax
import jax.numpy as jnp
import numpy as np
from jax import lax
from jax.experimental import pallas as pl
from jax.experimental.pallas import tpu as pltpu
from jax.sharding import PartitionSpec as P

N = 160
ZP = 3
N_FFT = 64
NBLK = 96
ATOM_DEV = 16
ATOMS = 1024
SHIFT = 52
BOX = 104
HALF = 56
F32 = jnp.float32
BF16 = jnp.bfloat16

lda_factor = (3.0 / math.pi) ** (1.0 / 3.0)


def parts(table):
    high = table.astype(np.float32).astype(jnp.bfloat16)
    low = (table - high.astype(np.float64)).astype(np.float32).astype(jnp.bfloat16)
    return high, low


def real_form(cosine, sine):
    return np.block([[cosine, -sine], [sine, cosine]])


def z_tables():
    slot, place = np.meshgrid(np.arange(8), np.arange(N_FFT), indexing="ij")
    out = np.zeros((N_FFT, 8, 2, N))
    g = np.arange(N)
    for f in range(N_FFT):
        for s in range(ZP):
            z = s * N_FFT + f
            if z < N:
                phase = 2 * np.pi / N * ((z * g) % N)
                c, d = np.cos(phase) / math.sqrt(N), np.sin(phase) / math.sqrt(N)
                out[f, s, 0], out[f, s, 1] = c, -d
                out[f, 3 + s, 0], out[f, 3 + s, 1] = d, c
    forward = out.reshape(N_FFT * 8, 2 * N)
    return forward, forward.T


def x_tables():
    rows = np.array([4 * k + g for g in range(4) for k in range(40)])
    compact = np.array([2 * h + p for p in range(2) for h in range(HALF)])
    phase = 2 * np.pi / N * ((rows[:, None] * (compact[None, :] - SHIFT)) % N)
    keep = (compact < BOX)[None, :] / math.sqrt(N)
    ahead = real_form(np.cos(phase) * keep, np.sin(phase) * keep)
    compact = np.arange(BOX)
    phase = 2 * np.pi / N * (((compact[:, None] - SHIFT) * rows[None, :]) % N)
    back = real_form(np.cos(phase) / math.sqrt(N), -np.sin(phase) / math.sqrt(N))
    return ahead, back


PAIRS = tuple((j, g) for g in range(4) for j in (g, g + 1))


def y_tables():
    compact = np.arange(128)
    out = []
    for j, g in PAIRS:
        flat = 128 * j + np.arange(128)
        keep = ((flat // N == g)[None, :] & (compact < BOX)[:, None]) / math.sqrt(N)
        phase = 2 * np.pi / N * (((compact[:, None] - SHIFT) * (flat % N)[None, :]) % N)
        c, d = np.cos(phase) * keep, np.sin(phase) * keep
        out.append(np.block([[c, d], [-d, c]]))
    return np.stack(out)


def stack3(table, axis):
    high, low = parts(table)
    return np.concatenate([high, low, high], axis=axis)


def make_tables():
    z_ahead, z_back = z_tables()
    x_ahead, x_back = x_tables()
    y_ahead = y_tables()
    y_back = np.swapaxes(y_ahead, 1, 2)
    return dict(
        z_ahead=stack3(z_ahead, 1),
        z_back=stack3(z_back, 1),
        x_ahead=stack3(x_ahead, 1),
        x_back=stack3(x_back, 1),
        y_ahead=np.stack(parts(y_ahead), axis=1),
        y_back=np.stack(parts(y_back), axis=1),
    )


def split(value):
    high = value.astype(BF16)
    return high, (value - high.astype(F32)).astype(BF16)


def dot(left, right):
    return lax.dot_general(left, right, (((1,), (0,)), ((), ())), preferred_element_type=F32)


def dot_nt(left, right):
    return lax.dot_general(left, right, (((1,), (1,)), ((), ())), preferred_element_type=F32)


def lhs3(value):
    high, low = split(value)
    return jnp.concatenate([high, high, low], axis=1)


def rhs3(value):
    high, low = split(value)
    return jnp.concatenate([high, high, low], axis=0)


def grid_xy(stick_ref):
    column = stick_ref[...].astype(F32)
    x = jnp.floor((column + 0.5) * (1.0 / N))
    y = column - N * x
    return x, y


def block_row(place):
    slot = (place >= 200).astype(jnp.int32) + (place >= 400).astype(jnp.int32)
    inside = place - 200 * slot
    fifth = (inside * 6554) >> 15
    return slot * 200 + (inside - 5 * fifth) * 40 + fifth


def z_forward(stick_ref, wave_ref, table_ref, out_ref):
    x, y = grid_xy(stick_ref)
    half = N // 2
    xc = jnp.where(x < half, x, x - N) + SHIFT
    yc = jnp.where(y < half, y, y - N) + SHIFT
    both = [jnp.concatenate([wave_ref[0, b], wave_ref[1, b]], axis=0) for b in range(2)]
    result = dot(table_ref[...], rhs3(jnp.concatenate(both, axis=1)))
    for b in range(2):
        out_ref[:, 8 * b : 8 * b + 8, :] = result[:, 128 * b : 128 * b + 128].reshape(N_FFT, 8, 128)
    out_ref[:, 6:7, :] = jnp.broadcast_to(xc[None], (N_FFT, 1, 128))
    out_ref[:, 7:8, :] = jnp.broadcast_to(yc[None], (N_FFT, 1, 128))


def z_backward(stick_ref, wave_ref, table_ref, back_ref, out_ref):
    both = [back_ref[:, 8 * b : 8 * b + 8, :].reshape(N_FFT * 8, 128) for b in range(2)]
    result = dot(table_ref[...], rhs3(jnp.concatenate(both, axis=1)))
    x, y = grid_xy(stick_ref)
    half = N // 2
    x = jnp.where(x < half, x, x - N) / N
    y = jnp.where(y < half, y, y - N) / N
    g = lax.broadcasted_iota(jnp.int32, (N, 128), 0)
    z = jnp.where(g < half, g, g - N).astype(F32) / N
    kinetic = 2.0 * (x * x + y * y) + 2.0 * (z * z)
    for o in range(2):
        for b in range(2):
            spectrum = result[N * o : N * o + N, 128 * b : 128 * b + 128]
            out_ref[o, b] = spectrum + kinetic * wave_ref[o, b]


ROWS = [(b, o, s) for b in range(2) for o in range(2) for s in range(ZP)]
CHUNK = 4


def to_planes(
    place_ref,
    atom_ref,
    occ_ref,
    sticks_ref,
    xtab_ref,
    ytab_hbm,
    proj_hbm,
    psi_ref,
    sums_ref,
    dens_ref,
    grid_ref,
    mid_ref,
    ytab_ref,
    proj_ref,
    acc_ref,
    power_ref,
    sems,
):
    ytab_copy = pltpu.make_async_copy(ytab_hbm, ytab_ref, sems.at[0])
    proj_copy = pltpu.make_async_copy(proj_hbm, proj_ref, sems.at[1])
    ytab_copy.start()
    proj_copy.start()

    grid_ref[...] = jnp.zeros_like(grid_ref)
    row_id = lax.broadcasted_iota(jnp.int32, (HALF, 128), 0).astype(F32)
    lane_id = lax.broadcasted_iota(jnp.int32, (256, 128), 0).astype(F32)

    def scatter(chunk, carry):
        lefts, rights = [], []
        for i in range(CHUNK):
            tile = sticks_ref[chunk * CHUNK + i]
            x, y = tile[6:7], tile[7:8]
            x2 = jnp.floor(x * 0.5)
            here = row_id == x2
            spot = (lane_id == (x - 2.0 * x2) * 128.0 + y).astype(F32).astype(BF16)
            high = tile.astype(BF16).astype(F32)
            low = tile - high
            for piece in (high, low):
                picked = [
                    jnp.where(here, piece[8 * b + 3 * o + s : 8 * b + 3 * o + s + 1], 0.0)
                    for b, o, s in ROWS
                ]
                lefts.append(jnp.concatenate(picked, axis=0).astype(BF16))
                rights.append(spot)
        grid_ref[...] += dot_nt(jnp.concatenate(lefts, axis=1), jnp.concatenate(rights, axis=1))
        return carry

    lax.fori_loop(0, N_FFT // CHUNK, scatter, 0)

    columns = []
    for b in range(2):
        for s in range(ZP):
            rows = []
            for o in range(2):
                first = (b * 6 + o * 3 + s) * HALF
                for parity in range(2):
                    rows.append(
                        grid_ref[first : first + HALF, 128 * parity : 128 * parity + 128]
                    )
            columns.append(jnp.concatenate(rows, axis=0))
    mixed = dot(xtab_ref[...], rhs3(jnp.concatenate(columns, axis=1)))
    for g in range(4):
        for o in range(2):
            first = (o * 4 + g) * 40
            for bs in range(6):
                mid_ref[g, 40 * bs : 40 * bs + 40, 128 * o : 128 * o + 128] = mixed[
                    first : first + 40, 128 * bs : 128 * bs + 128
                ]
    lefts = [lhs3(mid_ref[g]) for g in range(4)]
    ytab_copy.wait()
    for j in range(5):
        total = None
        for at, (tile, g) in enumerate(PAIRS):
            if tile == j:
                high, low = ytab_ref[at, 0], ytab_ref[at, 1]
                term = dot(lefts[g], jnp.concatenate([high, low, high], axis=0))
                total = term if total is None else total + term
        for b in range(2):
            for s in range(ZP):
                bs = b * ZP + s
                for o in range(2):
                    first = s * 200 + j * 40
                    psi_ref[b * 2 + o, first : first + 40, :] = total[
                        40 * bs : 40 * bs + 40, 128 * o : 128 * o + 128
                    ]

    def power(b):
        re, im = psi_ref[2 * b], psi_ref[2 * b + 1]
        return re * re + im * im

    power_ref[...] = (occ_ref[0] * power(0) + occ_ref[1] * power(1)).reshape(ZP, 200, 128)
    for q in range(200):
        row = (q % 5) * 40 + q // 5
        dens_ref[:, 128 * q : 128 * q + 128] = power_ref[:, row, :]

    acc_ref[...] = jnp.zeros_like(acc_ref)
    base = lax.axis_index("fft") * ATOM_DEV - ATOM_DEV // 2
    proj_copy.wait()

    def project(k, carry):
        row = block_row(place_ref[k])
        first = ((atom_ref[k] - base) & (ATOMS - 1)) * 4
        values = proj_ref[k]
        for c in range(4):
            acc_ref[first + c] += values * psi_ref[c, pl.ds(row, 1), :]
        return carry

    lax.fori_loop(0, NBLK, project, 0)
    ones = jnp.ones((256, 128), BF16)
    lane = lax.broadcasted_iota(jnp.int32, (64, 128), 1)
    sums = jnp.zeros((64, 128), F32)
    for chunk in range(8):
        high, low = split(acc_ref[16 * chunk : 16 * chunk + 16].reshape(1024, 128))
        total = dot(jnp.concatenate([high, low], axis=1), ones)
        for m in range(16):
            sums = jnp.where(lane == chunk * 16 + m, total[64 * m : 64 * m + 64], sums)
    sums_ref[...] = sums


def to_sticks(
    place_ref,
    atom_ref,
    sums_ref,
    before_ref,
    after_ref,
    coupling_ref,
    sticks_ref,
    psi_ref,
    potential_ref,
    xtab_ref,
    ytab_hbm,
    proj_hbm,
    out_ref,
    weight_ref,
    pot_ref,
    h_ref,
    plane_ref,
    left_ref,
    ytab_ref,
    proj_ref,
    sems,
):
    ytab_copy = pltpu.make_async_copy(ytab_hbm, ytab_ref, sems.at[0])
    proj_copy = pltpu.make_async_copy(proj_hbm, proj_ref, sems.at[1])
    proj_copy.start()
    ytab_copy.start()

    for q in range(200):
        row = (q % 5) * 40 + q // 5
        pot_ref[:, row, :] = potential_ref[:, 128 * q : 128 * q + 128]
    potential = pot_ref[...].reshape(600, 128)
    for c in range(4):
        h_ref[c] = potential * psi_ref[c]

    lane = lax.broadcasted_iota(jnp.int32, (64, 128), 1)
    beside = jnp.where(
        lane < 64, pltpu.roll(before_ref[...], 64, 1), pltpu.roll(after_ref[...], 64, 1)
    )
    combined = sums_ref[...] + beside
    weight = lax.dot_general(
        coupling_ref[...],
        combined,
        (((1,), (0,)), ((), ())),
        precision=lax.Precision.HIGHEST,
        preferred_element_type=F32,
    )
    for n in range(128):
        weight_ref[n] = jnp.broadcast_to(weight[:, n : n + 1], (64, 128))
    base = lax.axis_index("fft") * ATOM_DEV - ATOM_DEV // 2
    proj_copy.wait()

    def add(k, carry):
        row = block_row(place_ref[k])
        first = ((atom_ref[k] - base) & (ATOMS - 1)) * 4
        values = proj_ref[k]
        for c in range(4):
            h_ref[c, pl.ds(row, 1), :] += jnp.sum(
                values * weight_ref[first + c], axis=0, keepdims=True
            )
        return carry

    lax.fori_loop(0, NBLK, add, 0)

    lefts = []
    for j in range(5):
        rows = []
        for b in range(2):
            for s in range(ZP):
                first = s * 200 + j * 40
                rows.append(
                    jnp.concatenate(
                        [h_ref[b * 2 + o, first : first + 40, :] for o in range(2)], axis=1
                    )
                )
        lefts.append(lhs3(jnp.concatenate(rows, axis=0)))
    ytab_copy.wait()
    turned = []
    for g in range(4):
        total = None
        for at, (j, group) in enumerate(PAIRS):
            if group == g:
                high, low = ytab_ref[at, 0], ytab_ref[at, 1]
                term = dot(lefts[j], jnp.concatenate([high, low, high], axis=0))
                total = term if total is None else total + term
        turned.append(total)
    columns = []
    for bs in range(6):
        rows = []
        for o in range(2):
            for g in range(4):
                rows.append(turned[g][40 * bs : 40 * bs + 40, 128 * o : 128 * o + 128])
        columns.append(jnp.concatenate(rows, axis=0))
    spectrum = dot(xtab_ref[...], rhs3(jnp.concatenate(columns, axis=1)))
    for at, (b, o, s) in enumerate(ROWS):
        bs = b * ZP + s
        plane_ref[at * BOX : at * BOX + BOX, :] = spectrum[
            o * BOX : o * BOX + BOX, 128 * bs : 128 * bs + 128
        ]
    high, low = split(plane_ref[...])
    left_ref[:, :128] = high
    left_ref[:, 128:] = low

    row_id = lax.broadcasted_iota(jnp.int32, (128, 256), 0).astype(F32)
    zeros = jnp.zeros((2, 256), F32)

    def gather(pair, carry):
        one, two = sticks_ref[2 * pair], sticks_ref[2 * pair + 1]
        x = jnp.concatenate([one[6:7], two[6:7]], axis=1)
        y = jnp.concatenate([one[7:8], two[7:8]], axis=1)
        spot = (row_id == y).astype(F32).astype(BF16)
        values = dot(left_ref[...], jnp.concatenate([spot, spot], axis=0))
        here = row_id[:BOX] == x
        rows = []
        for at in range(12):
            masked = jnp.where(here, values[at * BOX : at * BOX + BOX], 0.0)
            rows.append(jnp.sum(masked, axis=0, keepdims=True))
            if at % 6 == 5:
                rows.append(zeros)
        result = jnp.concatenate(rows, axis=0)
        out_ref[2 * pair] = result[:, :128]
        out_ref[2 * pair + 1] = result[:, 128:]
        return carry

    lax.fori_loop(0, N_FFT // 2, gather, 0)


VMEM = pltpu.VMEM
SMEM_SPEC = pl.BlockSpec(memory_space=pltpu.SMEM)
VMEM_SPEC = pl.BlockSpec(memory_space=pltpu.VMEM)
ANY_SPEC = pl.BlockSpec(memory_space=pl.ANY)
LIMIT = 56 * 1024 * 1024


def call(body, in_specs, outs, scratch=(), flops=0, size=0):
    return pl.pallas_call(
        body,
        out_shape=outs,
        in_specs=in_specs,
        out_specs=jax.tree.map(lambda _: VMEM_SPEC, outs),
        scratch_shapes=list(scratch),
        compiler_params=pltpu.CompilerParams(vmem_limit_bytes=LIMIT),
        cost_estimate=pl.CostEstimate(flops=flops, bytes_accessed=size, transcendentals=0),
    )


def shape(*dims):
    return jax.ShapeDtypeStruct(dims, F32)


def make_calls():
    forward = call(z_forward, [VMEM_SPEC] * 3, shape(N_FFT, 16, 128), (), 500_000_000, 2_000_000)
    backward = call(z_backward, [VMEM_SPEC] * 4, shape(2, 2, N, 128), (), 500_000_000, 2_000_000)
    planes = call(
        to_planes,
        [SMEM_SPEC] * 3 + [VMEM_SPEC] * 2 + [ANY_SPEC] * 2,
        (shape(4, 600, 128), shape(64, 128), shape(ZP, N * N)),
        (
            VMEM((12 * HALF, 256), F32),
            VMEM((4, 240, 256), F32),
            VMEM((8, 2, 256, 256), BF16),
            VMEM((NBLK, 64, 128), F32),
            VMEM((128, 64, 128), F32),
            VMEM((ZP, 200, 128), F32),
            pltpu.SemaphoreType.DMA((2,)),
        ),
        10_000_000_000,
        8_000_000,
    )
    sticks = call(
        to_sticks,
        [SMEM_SPEC] * 2 + [VMEM_SPEC] * 8 + [ANY_SPEC] * 2,
        shape(N_FFT, 16, 128),
        (
            VMEM((128, 64, 128), F32),
            VMEM((ZP, 200, 128), F32),
            VMEM((4, 600, 128), F32),
            VMEM((12 * BOX, 128), F32),
            VMEM((12 * BOX, 256), BF16),
            VMEM((8, 2, 256, 256), BF16),
            VMEM((NBLK, 64, 128), F32),
            pltpu.SemaphoreType.DMA((2,)),
        ),
        10_000_000_000,
        8_000_000,
    )
    return forward, backward, planes, sticks


def local(
    tables,
    wave_coef,
    stick_map,
    local_potential,
    core_density,
    occupations,
    block_place,
    block_atom,
    projectors,
    coupling,
):
    forward, backward, planes, sticks = make_calls()
    fft_index = lax.axis_index("fft")
    stick_row = stick_map.reshape(1, 128)
    sent = forward(stick_row, wave_coef, tables["z_ahead"])
    arrived = lax.all_to_all(sent, "fft", split_axis=0, concat_axis=0, tiled=True)
    psi, sums, group_density = planes(
        block_place,
        block_atom,
        occupations,
        arrived,
        tables["x_ahead"],
        tables["y_ahead"],
        projectors,
    )
    density = lax.psum(group_density, "band")
    up = [(i, (i + 1) % N_FFT) for i in range(N_FFT)]
    down = [(j, i) for i, j in up]
    before = lax.ppermute(sums, "fft", up)
    after = lax.ppermute(sums, "fft", down)
    result = sticks(
        block_place,
        block_atom,
        sums,
        before,
        after,
        coupling,
        arrived,
        psi,
        local_potential,
        tables["x_back"],
        tables["y_back"],
        projectors,
    )
    returned = lax.all_to_all(result, "fft", split_axis=0, concat_axis=0, tiled=True)
    applied = backward(stick_row, wave_coef, tables["z_back"], returned)
    valid = (jnp.arange(ZP, dtype=jnp.int32) * N_FFT + fft_index < N).astype(F32)
    exchange_field = -lda_factor * jnp.cbrt(density + core_density) * valid[:, None]
    return (applied, density, exchange_field)


def solution(mesh):
    tables = {name: jnp.asarray(value) for name, value in make_tables().items()}

    def run(*args):
        return local(tables, *args)

    return jax.shard_map(
        run,
        mesh=mesh,
        in_specs=(
            P(None, "band", None, "fft"),
            P("fft"),
            P("fft", None),
            P("fft", None),
            P("band"),
            P("fft"),
            P("fft"),
            P("fft", None, None),
            P(),
        ),
        out_specs=(P(None, "band", None, "fft"), P("fft", None), P("fft", None)),
        check_vma=False,
    )
```

profile of v0, /device:TPU:1, one launch (start us, length us, event | category | flops | bytes accessed | tf_op | source)
XLA Modules:
  0.0 119.8 jit_solution(9128093596874649396)
XLA Ops:
  7.2 2.6 %shard_map.166 = f32[64,16,128]{2,1,0:T(8,128)} custom-call(s32[1,128]{1,0:T(1,128)} %bitcast.1, f32[2,2,160,128]{3,2,1,0:T(8,128)} %wave_ref.3, bf16[512,960]{1,0:T(8,128)(2,1)} %constant.24.clone.table_ref), custom_call_target="tpu_custom_call" | custom-call | flops 500000000 | bytes 2000000 | tf_op jit(solution)/shard_map/pallas_call | solution.py:493
  9.8 10.3 %all-to-all-start = ((f32[64,16,128]{2,1,0:T(8,128)}), f32[64,16,128]{2,1,0:T(8,128)S(1)}, u32[]{:S(2)}, u32[]{:S(2)}) async-start(f32[64,16,128]{2,1,0:T(8,128)} %shard_map.166), calls=%async_computation | async-start | bytes 1048576 | tf_op jit(solution)/shard_map/all_to_all | solution.py:494
  20.1 0.0 all-reduce.2.cloned.1.call-start
  20.2 12.4 %all-to-all-done.sticks_ref = f32[64,16,128]{2,1,0:T(8,128)S(1)} async-done(((f32[64,16,128]{2,1,0:T(8,128)}), f32[64,16,128]{2,1,0:T(8,128)S(1)}, u32[]{:S(2)}, u32[]{:S(2)}) %all-to-all-start) | async-done | bytes 524320 | tf_op jit(solution)/shard_map/all_to_all | solution.py:494
  32.6 0.0 copy-start.2
  32.6 0.8 copy-done.2
  33.3 17.0 %shard_map.167 = (f32[4,600,128]{2,1,0:T(8,128)}, f32[64,128]{1,0:T(8,128)}, f32[3,25600]{1,0:T(4,128)}) custom-call(s32[96]{0:T(128)} %place_ref.3, s32[96]{0:T(128)} %atom_ref.3, f32[2]{0:T(128)} %occ_ref.1, f32[64,16,128]{2,1,0:T(8,128)} %copy-done.2, bf16[320,672]{1,0:T(8,128)(2,1)} %constant.25.clone.xtab_ref, ...), custom_call_target="tpu_custom_call" | custom-call | flops 10000000000 | bytes 8000000 | tf_op jit(solution)/shard_map/pallas_call | solution.py:495
  50.4 0.8 collective-permute-start
  51.2 0.0 collective-permute-start.1
  51.2 0.0 all-reduce.2.cloned.1.call-update
  51.2 1.3 %collective-permute-done.before_ref = f32[64,128]{1,0:T(8,128)S(1)} collective-permute-done((f32[64,128]{1,0:T(8,128)}, f32[64,128]{1,0:T(8,128)S(1)}, u32[]{:S(2)}, u32[]{:S(2)}) %collective-permute-start) | collective-permute-done | bytes 32800 | tf_op jit(solution)/shard_map/ppermute | solution.py:507
  52.5 0.0 copy-start.4
  52.5 2.2 %collective-permute-done.1.after_ref = f32[64,128]{1,0:T(8,128)S(1)} collective-permute-done((f32[64,128]{1,0:T(8,128)}, f32[64,128]{1,0:T(8,128)S(1)}, u32[]{:S(2)}, u32[]{:S(2)}) %collective-permute-start.1) | collective-permute-done | bytes 32800 | tf_op jit(solution)/shard_map/ppermute | solution.py:508
  54.7 0.0 copy-start.5
  54.7 0.0 copy-done.4
  54.7 0.6 copy-done.5
  55.3 0.0 copy-start.3
  55.3 19.8 %shard_map.168 = f32[64,16,128]{2,1,0:T(8,128)} custom-call(s32[96]{0:T(128)} %place_ref.3, s32[96]{0:T(128)} %atom_ref.3, f32[64,128]{1,0:T(8,128)} %get-tuple-element.6.sums_ref, f32[64,128]{1,0:T(8,128)} %copy-done.4, f32[64,128]{1,0:T(8,128)} %copy-done.5, f32[64,64]{1,0:T(8,128)} %coupling_ref.1, f32[64,16,128]{2,1,0:T(8,128)} %copy-done.2, ...), custom_call_target="tpu_custom_call" | custom-call | flops 10000000000 | bytes 8000000 | tf_op jit(solution)/shard_map/pallas_call | solution.py:509
  75.2 11.8 %all-to-all-start.1 = ((f32[64,16,128]{2,1,0:T(8,128)}), f32[64,16,128]{2,1,0:T(8,128)S(1)}, u32[]{:S(2)}, u32[]{:S(2)}) async-start(f32[64,16,128]{2,1,0:T(8,128)} %shard_map.168), calls=%async_computation.1 | async-start | bytes 1048576 | tf_op jit(solution)/shard_map/all_to_all | solution.py:523
  86.9 19.4 %all-reduce.2.cloned.1.call-done = f32[3,25600]{1,0:T(4,128)} async-done(((f32[3,25600]{1,0:T(4,128)}), f32[3,25600]{1,0:T(4,128)}) %all-reduce.2.cloned.1.call-update) | async-done | bytes 307216 | tf_op jit(solution)/shard_map/psum | solution.py:504
  106.3 0.0 copy-done.3
  106.3 0.0 copy-start.1
  106.3 2.5 %cbrt_multiply_fusion = f32[3,25600]{1,0:T(4,128)} fusion(f32[3,25600]{1,0:T(4,128)} %all-reduce.2.cloned.1.call-done, f32[3,25600]{1,0:T(4,128)S(1)} %copy-done.3, f32[3]{0:T(128)S(1)} %compare_select_fusion), kind=kLoop, calls=%fused_computation | loop fusion | flops 153600 | bytes 921612 | tf_op jit(solution)/shard_map/mul | solution.py:526
  108.8 0.0 all-to-all-done.1.back_ref
  108.8 0.0 copy-start
  108.8 0.8 copy-done
  109.6 2.6 %shard_map.169 = f32[2,2,160,128]{3,2,1,0:T(8,128)} custom-call(s32[1,128]{1,0:T(1,128)} %bitcast.2, f32[2,2,160,128]{3,2,1,0:T(8,128)} %wave_ref.3, bf16[320,1536]{1,0:T(8,128)(2,1)} %constant.29.clone.table_ref, f32[64,16,128]{2,1,0:T(8,128)} %copy-done), custom_call_target="tpu_custom_call" | custom-call | flops 500000000 | bytes 2000000 | tf_op jit(solution)/shard_map/pallas_call | solution.py:524
  112.2 0.0 copy-done.1
  112.2 0.8 copy.19
  (1 shorter events, 0.0 us)
Async XLA Ops:
  9.8 22.8 %all-to-all-start = ((f32[64,16,128]{2,1,0:T(8,128)}), f32[64,16,128]{2,1,0:T(8,128)S(1)}, u32[]{:S(2)}, u32[]{:S(2)}) async-start(f32[64,16,128]{2,1,0:T(8,128)} %shard_map.166), calls=%async_computation | async-start | bytes 1048576 | tf_op jit(solution)/shard_map/all_to_all | solution.py:494
  20.1 86.2 %all-reduce.2.cloned.1.call-start = ((), (), s32[]{:S(2)}) async-start(), calls=%async_computation.2 | async-start | bytes 819200 | tf_op jit(solution)/shard_map/psum | solution.py:504
  32.6 0.8 copy-start.2
  50.4 2.1 %collective-permute-start = (f32[64,128]{1,0:T(8,128)}, f32[64,128]{1,0:T(8,128)S(1)}, u32[]{:S(2)}, u32[]{:S(2)}) collective-permute-start(f32[64,128]{1,0:T(8,128)} %get-tuple-element.6.sums_ref), channel_id=1, source_target_pairs={{0,1},{1,2},{2,3},{3,4},{4,5},{5,6},{6,7},{7,8},{8,9},{9,10},{10,1... | collective-permute-start | bytes 98312 | tf_op jit(solution)/shard_map/ppermute | solution.py:507
  51.2 3.6 %collective-permute-start.1 = (f32[64,128]{1,0:T(8,128)}, f32[64,128]{1,0:T(8,128)S(1)}, u32[]{:S(2)}, u32[]{:S(2)}) collective-permute-start(f32[64,128]{1,0:T(8,128)} %get-tuple-element.6.sums_ref), channel_id=1, source_target_pairs={{1,0},{2,1},{3,2},{4,3},{5,4},{6,5},{7,6},{8,7},{9,8},{10,9},{11,1... | collective-permute-start | bytes 98312 | tf_op jit(solution)/shard_map/ppermute | solution.py:508
  52.5 2.2 %copy-start.4 = (f32[64,128]{1,0:T(8,128)}, f32[64,128]{1,0:T(8,128)S(1)}, u32[]{:S(2)}) copy-start(f32[64,128]{1,0:T(8,128)S(1)} %collective-permute-done.before_ref) | copy-start | bytes 98308
  54.7 0.6 copy-start.5
  55.3 51.0 %copy-start.3 = (f32[3,25600]{1,0:T(4,128)S(1)}, f32[3,25600]{1,0:T(4,128)}, u32[]{:S(2)}) copy-start(f32[3,25600]{1,0:T(4,128)} %param.18) | copy-start | bytes 921604
  75.2 33.7 %all-to-all-start.1 = ((f32[64,16,128]{2,1,0:T(8,128)}), f32[64,16,128]{2,1,0:T(8,128)S(1)}, u32[]{:S(2)}, u32[]{:S(2)}) async-start(f32[64,16,128]{2,1,0:T(8,128)} %shard_map.168), calls=%async_computation.1 | async-start | bytes 1048576 | tf_op jit(solution)/shard_map/all_to_all | solution.py:523
  106.3 5.9 %copy-start.1 = (f32[3,25600]{1,0:T(4,128)S(1)}, f32[3,25600]{1,0:T(4,128)}, u32[]{:S(2)}) copy-start(f32[3,25600]{1,0:T(4,128)} %all-reduce.2.cloned.1.call-done) | copy-start | bytes 921604
  108.8 0.8 copy-start
Sparse Core Ops, SparseCore 0:
  51.3 54.9 all-reduce.1
where the time goes:
time: 120 us
  Pallas kernels  42 us (35%)
  waiting for transfers between devices  35.3 us (29%)
  starting transfers between devices  23 us (19%)
  between operations  14.1 us (12%)
  local copies, waits for them, and re-layouts  2.95 us (2%)
  other arithmetic  2.5 us (2%)
    pallas_call x1, Pallas kernels, local(): sticks(block_place, block_atom, sums, before, after, coupling, arrived, p...  19.8 us
    psum x1, waiting for transfers between devices, local(): density = lax.psum(group_density, 'band')  19.4 us
    pallas_call x1, Pallas kernels, local(): planes(block_place, block_atom, occupations, arrived, tables['x_ahead'],...  17 us
    all_to_all x1, waiting for transfers between devices, local(): lax.all_to_all(sent, 'fft', split_axis=0, concat_axis=0, tiled=True)  12.4 us
    all_to_all x1, starting transfers between devices, local(): lax.all_to_all(result, 'fft', split_axis=0, concat_axis=0, tiled=True)  11.8 us
    all_to_all x1, starting transfers between devices, local(): lax.all_to_all(sent, 'fft', split_axis=0, concat_axis=0, tiled=True)  10.3 us
    unnamed x13, local copies, waits for them, and re-layouts  2.95 us
    pallas_call x1, Pallas kernels, local(): applied = backward(stick_row, wave_coef, tables['z_back'], returned)  2.6 us
  transfers between devices with their start and end apart: 5, of which 4 were waited for; matrix products, arithmetic and copies ran while one was open for 2% of the time, Pallas kernels for 17%

commit v1 on v0

--- a/solution.py
+++ b/solution.py
@@ -14,6 +14,8 @@
 NBLK = 96
 ATOM_DEV = 16
 ATOMS = 1024
+BANDS_AXIS = 4
+SLICE = 152
 SHIFT = 52
 BOX = 104
 HALF = 56
@@ -133,62 +135,116 @@
     return slot * 200 + (inside - 5 * fifth) * 40 + fifth
 
 
-def z_forward(stick_ref, wave_ref, table_ref, out_ref):
+def shifted(me, step, sign):
+    def digit(value, unit, size):
+        return lax.rem(lax.div(value, unit), size)
+
+    core = lax.rem(digit(me, 1, 2) + digit(step, 1, 2), 2)
+    y = lax.rem(digit(me, 2, 4) + sign * digit(step, 2, 4) + 4, 4)
+    z = lax.rem(digit(me, 8, 2) + digit(step, 8, 2), 2)
+    x = lax.rem(digit(me, 16, 4) + sign * digit(step, 16, 4) + 4, 4)
+    return ((x * 2 + z) * 4 + y) * 2 + core
+
+
+ROWS = [(b, o, s) for b in range(2) for o in range(2) for s in range(ZP)]
+CHUNK = 4
+
+
+def exchange_copy(send_ref, land_ref, send_sems, recv_sems, me, step):
+    target = shifted(me, step, 1)
+    return pltpu.make_async_remote_copy(
+        src_ref=send_ref.at[target],
+        dst_ref=land_ref.at[me],
+        send_sem=send_sems.at[step],
+        recv_sem=recv_sems.at[step],
+        device_id={"fft": target},
+        device_id_type=pl.DeviceIdType.MESH,
+    )
+
+
+def landing(send_ref, land_ref, send_sems, recv_sems, me, step):
+    source = shifted(me, step, -1)
+    return pltpu.make_async_remote_copy(
+        src_ref=send_ref.at[source],
+        dst_ref=land_ref.at[source],
+        send_sem=send_sems.at[step],
+        recv_sem=recv_sems.at[step],
+        device_id={"fft": source},
+        device_id_type=pl.DeviceIdType.MESH,
+    )
+
+
+def greet(barrier, me):
+    def one(step, carry):
+        pl.semaphore_signal(
+            barrier,
+            inc=1,
+            device_id={"fft": shifted(me, step, 1)},
+            device_id_type=pl.DeviceIdType.MESH,
+        )
+        return carry
+
+    lax.fori_loop(1, N_FFT, one, 0)
+
+
+def to_planes(
+    occ_ref,
+    stick_ref,
+    wave_hbm,
+    ztab_hbm,
+    xtab_hbm,
+    ytab_hbm,
+    psi_ref,
+    power_ref,
+    xs_ref,
+    ys_ref,
+    wave_ref,
+    ztab_ref,
+    xtab_ref,
+    ytab_ref,
+    send_ref,
+    land_ref,
+    grid_ref,
+    mid_ref,
+    sems,
+    send_sems,
+    recv_sems,
+):
+    me = lax.axis_index("fft")
+    loads = [
+        pltpu.make_async_copy(source, target, sems.at[i])
+        for i, (source, target) in enumerate(
+            [(wave_hbm, wave_ref), (ztab_hbm, ztab_ref), (xtab_hbm, xtab_ref), (ytab_hbm, ytab_ref)]
+        )
+    ]
+    for load in loads:
+        load.start()
+    barrier = pltpu.get_barrier_semaphore()
+    greet(barrier, me)
+    loads[0].wait()
+    loads[1].wait()
+
     x, y = grid_xy(stick_ref)
     half = N // 2
     xc = jnp.where(x < half, x, x - N) + SHIFT
     yc = jnp.where(y < half, y, y - N) + SHIFT
     both = [jnp.concatenate([wave_ref[0, b], wave_ref[1, b]], axis=0) for b in range(2)]
-    result = dot(table_ref[...], rhs3(jnp.concatenate(both, axis=1)))
+    result = dot(ztab_ref[...], rhs3(jnp.concatenate(both, axis=1)))
     for b in range(2):
-        out_ref[:, 8 * b : 8 * b + 8, :] = result[:, 128 * b : 128 * b + 128].reshape(N_FFT, 8, 128)
-    out_ref[:, 6:7, :] = jnp.broadcast_to(xc[None], (N_FFT, 1, 128))
-    out_ref[:, 7:8, :] = jnp.broadcast_to(yc[None], (N_FFT, 1, 128))
-
-
-def z_backward(stick_ref, wave_ref, table_ref, back_ref, out_ref):
-    both = [back_ref[:, 8 * b : 8 * b + 8, :].reshape(N_FFT * 8, 128) for b in range(2)]
-    result = dot(table_ref[...], rhs3(jnp.concatenate(both, axis=1)))
-    x, y = grid_xy(stick_ref)
-    half = N // 2
-    x = jnp.where(x < half, x, x - N) / N
-    y = jnp.where(y < half, y, y - N) / N
-    g = lax.broadcasted_iota(jnp.int32, (N, 128), 0)
-    z = jnp.where(g < half, g, g - N).astype(F32) / N
-    kinetic = 2.0 * (x * x + y * y) + 2.0 * (z * z)
-    for o in range(2):
-        for b in range(2):
-            spectrum = result[N * o : N * o + N, 128 * b : 128 * b + 128]
-            out_ref[o, b] = spectrum + kinetic * wave_ref[o, b]
-
-
-ROWS = [(b, o, s) for b in range(2) for o in range(2) for s in range(ZP)]
-CHUNK = 4
-
-
-def to_planes(
-    place_ref,
-    atom_ref,
-    occ_ref,
-    sticks_ref,
-    xtab_ref,
-    ytab_hbm,
-    proj_hbm,
-    psi_ref,
-    sums_ref,
-    dens_ref,
-    grid_ref,
-    mid_ref,
-    ytab_ref,
-    proj_ref,
-    acc_ref,
-    power_ref,
-    sems,
-):
-    ytab_copy = pltpu.make_async_copy(ytab_hbm, ytab_ref, sems.at[0])
-    proj_copy = pltpu.make_async_copy(proj_hbm, proj_ref, sems.at[1])
-    ytab_copy.start()
-    proj_copy.start()
+        send_ref[:, 8 * b : 8 * b + 8, :] = result[:, 128 * b : 128 * b + 128].reshape(
+            N_FFT, 8, 128
+        )
+    send_ref[:, 6:7, :] = jnp.broadcast_to(xc[None], (N_FFT, 1, 128))
+    send_ref[:, 7:8, :] = jnp.broadcast_to(yc[None], (N_FFT, 1, 128))
+
+    pl.semaphore_wait(barrier, N_FFT - 1)
+
+    def send(step, carry):
+        exchange_copy(send_ref, land_ref, send_sems, recv_sems, me, step).start()
+        return carry
+
+    lax.fori_loop(1, N_FFT, send, 0)
+    land_ref[me] = send_ref[me]
 
     grid_ref[...] = jnp.zeros_like(grid_ref)
     row_id = lax.broadcasted_iota(jnp.int32, (HALF, 128), 0).astype(F32)
@@ -197,7 +253,13 @@
     def scatter(chunk, carry):
         lefts, rights = [], []
         for i in range(CHUNK):
-            tile = sticks_ref[chunk * CHUNK + i]
+            step = chunk * CHUNK + i
+
+            @pl.when(step > 0)
+            def _():
+                landing(send_ref, land_ref, send_sems, recv_sems, me, step).wait_recv()
+
+            tile = land_ref[shifted(me, step, -1)]
             x, y = tile[6:7], tile[7:8]
             x2 = jnp.floor(x * 0.5)
             here = row_id == x2
@@ -215,6 +277,8 @@
         return carry
 
     lax.fori_loop(0, N_FFT // CHUNK, scatter, 0)
+    xs_ref[...] = land_ref[:, 6, :]
+    ys_ref[...] = land_ref[:, 7, :]
 
     columns = []
     for b in range(2):
@@ -227,6 +291,7 @@
                         grid_ref[first : first + HALF, 128 * parity : 128 * parity + 128]
                     )
             columns.append(jnp.concatenate(rows, axis=0))
+    loads[2].wait()
     mixed = dot(xtab_ref[...], rhs3(jnp.concatenate(columns, axis=1)))
     for g in range(4):
         for o in range(2):
@@ -236,7 +301,7 @@
                     first : first + 40, 128 * bs : 128 * bs + 128
                 ]
     lefts = [lhs3(mid_ref[g]) for g in range(4)]
-    ytab_copy.wait()
+    loads[3].wait()
     for j in range(5):
         total = None
         for at, (tile, g) in enumerate(PAIRS):
@@ -257,16 +322,24 @@
         re, im = psi_ref[2 * b], psi_ref[2 * b + 1]
         return re * re + im * im
 
-    power_ref[...] = (occ_ref[0] * power(0) + occ_ref[1] * power(1)).reshape(ZP, 200, 128)
-    for q in range(200):
-        row = (q % 5) * 40 + q // 5
-        dens_ref[:, 128 * q : 128 * q + 128] = power_ref[:, row, :]
-
+    power_ref[:600] = occ_ref[0] * power(0) + occ_ref[1] * power(1)
+    power_ref[600:] = jnp.zeros((4 * SLICE - 600, 128), F32)
+
+    def sent(step, carry):
+        exchange_copy(send_ref, land_ref, send_sems, recv_sems, me, step).wait_send()
+        return carry
+
+    lax.fori_loop(1, N_FFT, sent, 0)
+
+
+def project(place_ref, atom_ref, psi_ref, proj_hbm, sums_ref, proj_ref, acc_ref, sems):
+    proj_copy = pltpu.make_async_copy(proj_hbm, proj_ref, sems.at[0])
+    proj_copy.start()
     acc_ref[...] = jnp.zeros_like(acc_ref)
     base = lax.axis_index("fft") * ATOM_DEV - ATOM_DEV // 2
     proj_copy.wait()
 
-    def project(k, carry):
+    def one(k, carry):
         row = block_row(place_ref[k])
         first = ((atom_ref[k] - base) & (ATOMS - 1)) * 4
         values = proj_ref[k]
@@ -274,7 +347,7 @@
             acc_ref[first + c] += values * psi_ref[c, pl.ds(row, 1), :]
         return carry
 
-    lax.fori_loop(0, NBLK, project, 0)
+    lax.fori_loop(0, NBLK, one, 0)
     ones = jnp.ones((256, 128), BF16)
     lane = lax.broadcasted_iota(jnp.int32, (64, 128), 1)
     sums = jnp.zeros((64, 128), F32)
@@ -286,34 +359,24 @@
     sums_ref[...] = sums
 
 
-def to_sticks(
+def apply_local(
     place_ref,
     atom_ref,
     sums_ref,
     before_ref,
     after_ref,
     coupling_ref,
-    sticks_ref,
     psi_ref,
     potential_ref,
-    xtab_ref,
-    ytab_hbm,
     proj_hbm,
-    out_ref,
+    h_ref,
     weight_ref,
     pot_ref,
-    h_ref,
-    plane_ref,
-    left_ref,
-    ytab_ref,
     proj_ref,
     sems,
 ):
-    ytab_copy = pltpu.make_async_copy(ytab_hbm, ytab_ref, sems.at[0])
-    proj_copy = pltpu.make_async_copy(proj_hbm, proj_ref, sems.at[1])
+    proj_copy = pltpu.make_async_copy(proj_hbm, proj_ref, sems.at[0])
     proj_copy.start()
-    ytab_copy.start()
-
     for q in range(200):
         row = (q % 5) * 40 + q // 5
         pot_ref[:, row, :] = potential_ref[:, 128 * q : 128 * q + 128]
@@ -349,6 +412,71 @@
         return carry
 
     lax.fori_loop(0, NBLK, add, 0)
+
+
+def slice_copy(source, target, send_sems, recv_sems, at, device):
+    return pltpu.make_async_remote_copy(
+        src_ref=source,
+        dst_ref=target,
+        send_sem=send_sems.at[at],
+        recv_sem=recv_sems.at[at],
+        device_id={"band": device},
+        device_id_type=pl.DeviceIdType.MESH,
+    )
+
+
+def to_sticks(
+    xs_ref,
+    ys_ref,
+    stick_ref,
+    h_ref,
+    power_ref,
+    core_ref,
+    wave_hbm,
+    ztab_hbm,
+    xtab_hbm,
+    ytab_hbm,
+    out_ref,
+    dens_ref,
+    field_ref,
+    wave_ref,
+    ztab_ref,
+    xtab_ref,
+    ytab_ref,
+    send_ref,
+    land_ref,
+    plane_ref,
+    left_ref,
+    part_ref,
+    full_ref,
+    mine_ref,
+    box_ref,
+    core3_ref,
+    sems,
+    send_sems,
+    recv_sems,
+    band_send_sems,
+    band_recv_sems,
+):
+    me = lax.axis_index("fft")
+    group = lax.axis_index("band")
+    loads = [
+        pltpu.make_async_copy(source, target, sems.at[i])
+        for i, (source, target) in enumerate(
+            [(ytab_hbm, ytab_ref), (xtab_hbm, xtab_ref), (wave_hbm, wave_ref), (ztab_hbm, ztab_ref)]
+        )
+    ]
+    for load in loads:
+        load.start()
+    barrier = pltpu.get_barrier_semaphore()
+    for step in range(1, 4):
+        pl.semaphore_signal(
+            barrier,
+            inc=1,
+            device_id={"band": lax.rem(group + step, 4)},
+            device_id_type=pl.DeviceIdType.MESH,
+        )
+    greet(barrier, me)
 
     lefts = []
     for j in range(5):
@@ -362,16 +490,36 @@
                     )
                 )
         lefts.append(lhs3(jnp.concatenate(rows, axis=0)))
-    ytab_copy.wait()
+    loads[0].wait()
     turned = []
     for g in range(4):
         total = None
-        for at, (j, group) in enumerate(PAIRS):
-            if group == g:
+        for at, (j, owner) in enumerate(PAIRS):
+            if owner == g:
                 high, low = ytab_ref[at, 0], ytab_ref[at, 1]
                 term = dot(lefts[j], jnp.concatenate([high, low, high], axis=0))
                 total = term if total is None else total + term
         turned.append(total)
+
+    pl.semaphore_wait(barrier, N_FFT - 1 + 3)
+
+    def rows_of(index):
+        return pl.ds(pl.multiple_of(index * SLICE, 8), SLICE)
+
+    def quarter(step):
+        target = lax.rem(group + step, 4)
+        return slice_copy(
+            power_ref.at[rows_of(target)],
+            part_ref.at[step - 1],
+            band_send_sems,
+            band_recv_sems,
+            step - 1,
+            target,
+        )
+
+    for step in range(1, 4):
+        quarter(step).start()
+
     columns = []
     for bs in range(6):
         rows = []
@@ -379,6 +527,7 @@
             for g in range(4):
                 rows.append(turned[g][40 * bs : 40 * bs + 40, 128 * o : 128 * o + 128])
         columns.append(jnp.concatenate(rows, axis=0))
+    loads[1].wait()
     spectrum = dot(xtab_ref[...], rhs3(jnp.concatenate(columns, axis=1)))
     for at, (b, o, s) in enumerate(ROWS):
         bs = b * ZP + s
@@ -393,9 +542,10 @@
     zeros = jnp.zeros((2, 256), F32)
 
     def gather(pair, carry):
-        one, two = sticks_ref[2 * pair], sticks_ref[2 * pair + 1]
-        x = jnp.concatenate([one[6:7], two[6:7]], axis=1)
-        y = jnp.concatenate([one[7:8], two[7:8]], axis=1)
+        steps = (2 * pair, 2 * pair + 1)
+        targets = [shifted(me, step, 1) for step in steps]
+        x = jnp.concatenate([xs_ref[pl.ds(t, 1), :] for t in targets], axis=1)
+        y = jnp.concatenate([ys_ref[pl.ds(t, 1), :] for t in targets], axis=1)
         spot = (row_id == y).astype(F32).astype(BF16)
         values = dot(left_ref[...], jnp.concatenate([spot, spot], axis=0))
         here = row_id[:BOX] == x
@@ -406,28 +556,113 @@
             if at % 6 == 5:
                 rows.append(zeros)
         result = jnp.concatenate(rows, axis=0)
-        out_ref[2 * pair] = result[:, :128]
-        out_ref[2 * pair + 1] = result[:, 128:]
+        send_ref[targets[0]] = result[:, :128]
+        send_ref[targets[1]] = result[:, 128:]
+
+        @pl.when(pair > 0)
+        def _():
+            exchange_copy(send_ref, land_ref, send_sems, recv_sems, me, steps[0]).start()
+
+        exchange_copy(send_ref, land_ref, send_sems, recv_sems, me, steps[1]).start()
         return carry
 
-    lax.fori_loop(0, N_FFT // 2, gather, 0)
+    lax.fori_loop(0, N_FFT // 4, gather, 0)
+
+    for step in range(1, 4):
+        quarter(step).wait()
+    mine = power_ref[rows_of(group)]
+    mine_ref[...] = mine + part_ref[0] + part_ref[1] + part_ref[2]
+    full_ref[rows_of(group)] = mine_ref[...]
+
+    def whole(step):
+        return slice_copy(
+            mine_ref,
+            full_ref.at[rows_of(group)],
+            band_send_sems,
+            band_recv_sems,
+            2 + step,
+            lax.rem(group + step, 4),
+        )
+
+    for step in range(1, 4):
+        whole(step).start()
+
+    lax.fori_loop(N_FFT // 4, N_FFT // 2, gather, 0)
+    land_ref[me] = send_ref[me]
+
+    for q in range(200):
+        row = (q % 5) * 40 + q // 5
+        core3_ref[:, row, :] = core_ref[:, 128 * q : 128 * q + 128]
+    for step in range(1, 4):
+        source = lax.rem(group + 4 - step, 4)
+        slice_copy(
+            mine_ref,
+            full_ref.at[rows_of(source)],
+            band_send_sems,
+            band_recv_sems,
+            2 + step,
+            source,
+        ).wait_recv()
+    for step in range(1, 4):
+        whole(step).wait_send()
+    density = full_ref[:600].reshape(ZP, 200, 128)
+    box_ref[...] = density
+    for q in range(200):
+        row = (q % 5) * 40 + q // 5
+        dens_ref[:, 128 * q : 128 * q + 128] = box_ref[:, row, :]
+    slot = lax.broadcasted_iota(jnp.int32, (ZP, 200, 128), 0)
+    field = -lda_factor * jnp.exp(jnp.log(density + core3_ref[...]) * (1.0 / 3.0))
+    core3_ref[...] = jnp.where(slot * N_FFT + me < N, field, 0.0)
+    for q in range(200):
+        row = (q % 5) * 40 + q // 5
+        field_ref[:, 128 * q : 128 * q + 128] = core3_ref[:, row, :]
+
+    loads[2].wait()
+    x, y = grid_xy(stick_ref)
+    half = N // 2
+    x = jnp.where(x < half, x, x - N) / N
+    y = jnp.where(y < half, y, y - N) / N
+    g = lax.broadcasted_iota(jnp.int32, (N, 128), 0)
+    z = jnp.where(g < half, g, g - N).astype(F32) / N
+    kinetic = 2.0 * (x * x + y * y) + 2.0 * (z * z)
+    loads[3].wait()
+
+    def arrive(step, carry):
+        landing(send_ref, land_ref, send_sems, recv_sems, me, step).wait_recv()
+        return carry
+
+    lax.fori_loop(1, N_FFT, arrive, 0)
+    both = [land_ref[:, 8 * b : 8 * b + 8, :].reshape(N_FFT * 8, 128) for b in range(2)]
+    result = dot(ztab_ref[...], rhs3(jnp.concatenate(both, axis=1)))
+    for o in range(2):
+        for b in range(2):
+            spectrum = result[N * o : N * o + N, 128 * b : 128 * b + 128]
+            out_ref[o, b] = spectrum + kinetic * wave_ref[o, b]
+
+    def sent(step, carry):
+        exchange_copy(send_ref, land_ref, send_sems, recv_sems, me, step).wait_send()
+        return carry
+
+    lax.fori_loop(1, N_FFT, sent, 0)
 
 
 VMEM = pltpu.VMEM
+DMA = pltpu.SemaphoreType.DMA
 SMEM_SPEC = pl.BlockSpec(memory_space=pltpu.SMEM)
 VMEM_SPEC = pl.BlockSpec(memory_space=pltpu.VMEM)
 ANY_SPEC = pl.BlockSpec(memory_space=pl.ANY)
 LIMIT = 56 * 1024 * 1024
 
 
-def call(body, in_specs, outs, scratch=(), flops=0, size=0):
+def call(body, in_specs, outs, scratch=(), flops=0, size=0, remote=None):
+    options = {} if remote is None else dict(collective_id=remote, has_side_effects=True)
     return pl.pallas_call(
         body,
         out_shape=outs,
         in_specs=in_specs,
         out_specs=jax.tree.map(lambda _: VMEM_SPEC, outs),
         scratch_shapes=list(scratch),
-        compiler_params=pltpu.CompilerParams(vmem_limit_bytes=LIMIT),
+        compiler_params=pltpu.CompilerParams(vmem_limit_bytes=LIMIT, **options),
         cost_estimate=pl.CostEstimate(flops=flops, bytes_accessed=size, transcendentals=0),
     )
 
@@ -437,42 +672,80 @@
 
 
 def make_calls():
-    forward = call(z_forward, [VMEM_SPEC] * 3, shape(N_FFT, 16, 128), (), 500_000_000, 2_000_000)
-    backward = call(z_backward, [VMEM_SPEC] * 4, shape(2, 2, N, 128), (), 500_000_000, 2_000_000)
+    wave = VMEM((2, 2, N, 128), F32)
+    ytab = VMEM((8, 2, 256, 256), BF16)
+    tiles = VMEM((N_FFT, 16, 128), F32)
     planes = call(
         to_planes,
-        [SMEM_SPEC] * 3 + [VMEM_SPEC] * 2 + [ANY_SPEC] * 2,
-        (shape(4, 600, 128), shape(64, 128), shape(ZP, N * N)),
+        [SMEM_SPEC, VMEM_SPEC] + [ANY_SPEC] * 4,
+        (shape(4, 600, 128), shape(4 * SLICE, 128), shape(N_FFT, 128), shape(N_FFT, 128)),
         (
+            wave,
+            VMEM((8 * N_FFT, 6 * N), BF16),
+            VMEM((2 * N, 12 * HALF), BF16),
+            ytab,
+            tiles,
+            tiles,
             VMEM((12 * HALF, 256), F32),
             VMEM((4, 240, 256), F32),
-            VMEM((8, 2, 256, 256), BF16),
-            VMEM((NBLK, 64, 128), F32),
-            VMEM((128, 64, 128), F32),
-            VMEM((ZP, 200, 128), F32),
-            pltpu.SemaphoreType.DMA((2,)),
+            DMA((4,)),
+            DMA((N_FFT,)),
+            DMA((N_FFT,)),
         ),
         10_000_000_000,
         8_000_000,
-    )
-    sticks = call(
-        to_sticks,
-        [SMEM_SPEC] * 2 + [VMEM_SPEC] * 8 + [ANY_SPEC] * 2,
-        shape(N_FFT, 16, 128),
+        0,
+    )
+    projected = call(
+        project,
+        [SMEM_SPEC] * 2 + [VMEM_SPEC, ANY_SPEC],
+        shape(64, 128),
+        (VMEM((NBLK, 64, 128), F32), VMEM((128, 64, 128), F32), DMA((1,))),
+        1_000_000_000,
+        8_000_000,
+    )
+    applied = call(
+        apply_local,
+        [SMEM_SPEC] * 2 + [VMEM_SPEC] * 6 + [ANY_SPEC],
+        shape(4, 600, 128),
         (
             VMEM((128, 64, 128), F32),
             VMEM((ZP, 200, 128), F32),
-            VMEM((4, 600, 128), F32),
+            VMEM((NBLK, 64, 128), F32),
+            DMA((1,)),
+        ),
+        1_000_000_000,
+        8_000_000,
+    )
+    sticks = call(
+        to_sticks,
+        [VMEM_SPEC] * 6 + [ANY_SPEC] * 4,
+        (shape(2, 2, N, 128), shape(ZP, N * N), shape(ZP, N * N)),
+        (
+            wave,
+            VMEM((2 * N, 24 * N_FFT), BF16),
+            VMEM((2 * BOX, 6 * N), BF16),
+            ytab,
+            tiles,
+            tiles,
             VMEM((12 * BOX, 128), F32),
             VMEM((12 * BOX, 256), BF16),
-            VMEM((8, 2, 256, 256), BF16),
-            VMEM((NBLK, 64, 128), F32),
-            pltpu.SemaphoreType.DMA((2,)),
+            VMEM((3, SLICE, 128), F32),
+            VMEM((4 * SLICE, 128), F32),
+            VMEM((SLICE, 128), F32),
+            VMEM((ZP, 200, 128), F32),
+            VMEM((ZP, 200, 128), F32),
+            DMA((4,)),
+            DMA((N_FFT,)),
+            DMA((N_FFT,)),
+            DMA((6,)),
+            DMA((6,)),
         ),
         10_000_000_000,
         8_000_000,
-    )
-    return forward, backward, planes, sticks
+        1,
+    )
+    return planes, projected, applied, sticks
 
 
 def local(
@@ -487,44 +760,36 @@
     projectors,
     coupling,
 ):
-    forward, backward, planes, sticks = make_calls()
-    fft_index = lax.axis_index("fft")
+    planes, projected, applied, sticks = make_calls()
     stick_row = stick_map.reshape(1, 128)
-    sent = forward(stick_row, wave_coef, tables["z_ahead"])
-    arrived = lax.all_to_all(sent, "fft", split_axis=0, concat_axis=0, tiled=True)
-    psi, sums, group_density = planes(
-        block_place,
-        block_atom,
+    psi, power, xs, ys = planes(
         occupations,
-        arrived,
+        stick_row,
+        wave_coef,
+        tables["z_ahead"],
         tables["x_ahead"],
         tables["y_ahead"],
-        projectors,
-    )
-    density = lax.psum(group_density, "band")
+    )
+    sums = projected(block_place, block_atom, psi, projectors)
     up = [(i, (i + 1) % N_FFT) for i in range(N_FFT)]
     down = [(j, i) for i, j in up]
     before = lax.ppermute(sums, "fft", up)
     after = lax.ppermute(sums, "fft", down)
-    result = sticks(
-        block_place,
-        block_atom,
-        sums,
-        before,
-        after,
-        coupling,
-        arrived,
-        psi,
-        local_potential,
+    h = applied(
+        block_place, block_atom, sums, before, after, coupling, psi, local_potential, projectors
+    )
+    return sticks(
+        xs,
+        ys,
+        stick_row,
+        h,
+        power,
+        core_density,
+        wave_coef,
+        tables["z_back"],
         tables["x_back"],
         tables["y_back"],
-        projectors,
-    )
-    returned = lax.all_to_all(result, "fft", split_axis=0, concat_axis=0, tiled=True)
-    applied = backward(stick_row, wave_coef, tables["z_back"], returned)
-    valid = (jnp.arange(ZP, dtype=jnp.int32) * N_FFT + fft_index < N).astype(F32)
-    exchange_field = -lda_factor * jnp.cbrt(density + core_density) * valid[:, None]
-    return (applied, density, exchange_field)
+    )
 
 
 def solution(mesh):

time: 120 us -> 95.6 us (0.80)
  Pallas kernels: 42 us -> 84.4 us
  waiting for transfers between devices: 35.3 us -> 1.81 us
  starting transfers between devices: 23 us -> 1.82 us
  between operations: 14.1 us -> 0.67 us
  local copies, waits for them, and re-layouts: 2.95 us -> 6.59 us
  other arithmetic: 2.5 us -> 0 us
    pallas_call x4, Pallas kernels: 42 us -> 84.4 us  [the longest x1 40.2 us: local(): sticks(xs, ys, stick_row, h, power, core_density, wave_coef, tables['z_ba...]
    all_to_all x2 -> x0, starting transfers between devices: 22.1 us -> none  [the longest x1 11.8 us: local(): lax.all_to_all(result, 'fft', split_axis=0, concat_axis=0, tiled=True)]
    psum x1 -> x0, waiting for transfers between devices: 19.4 us -> none  [local(): density = lax.psum(group_density, 'band')]
    all_to_all x2 -> x0, waiting for transfers between devices: 12.4 us -> none  [the longest x1 12.4 us: local(): lax.all_to_all(sent, 'fft', split_axis=0, concat_axis=0, tiled=True)]
    unnamed x13 -> x7, local copies, waits for them, and re-layouts: 2.95 us -> 6.59 us
    mul x2 -> x0, other arithmetic: 2.5 us -> none  [local(): -lda_factor * jnp.cbrt(density + core_density) * valid[:, None]]
    ppermute x1, waiting for transfers between devices: 1.31 us -> 0.01 us  [local(): before = lax.ppermute(sums, 'fft', up)]
  transfers between devices with their start and end apart: 5 -> 2, of which waited for: 4 -> 1; matrix products, arithmetic and copies ran while one was open for 2% -> 0% of each run, Pallas kernels for 17% -> 0%
where the time goes in v1:
time: 95.6 us; the launch traced here: 95.3 us
  Pallas kernels  84.4 us (88%)
  local copies, waits for them, and re-layouts  6.59 us (7%)
  starting transfers between devices  1.82 us (2%)
  waiting for transfers between devices  1.81 us (2%)
    pallas_call x1, Pallas kernels, local(): sticks(xs, ys, stick_row, h, power, core_density, wave_coef, tables['z_ba...  40.2 us
    pallas_call x1, Pallas kernels, local(): planes(occupations, stick_row, wave_coef, tables['z_ahead'], tables['x_ah...  29.4 us
    pallas_call x1, Pallas kernels, local(): sums = projected(block_place, block_atom, psi, projectors)  7.6 us
    pallas_call x1, Pallas kernels, local(): applied(block_place, block_atom, sums, before, after, coupling, psi, loca...  7.12 us
    unnamed x7, local copies, waits for them, and re-layouts  6.59 us
  transfers between devices with their start and end apart: 2, of which 1 were waited for; matrix products, arithmetic and copies ran while one was open for 0% of the time, Pallas kernels for 0%

profile of v1, /device:TPU:1, one launch (start us, length us, event | category | flops | bytes accessed | tf_op | source)
XLA Modules:
  0.0 95.3 jit_solution(901464929647557614)
XLA Ops:
  0.6 29.4 %shard_map.166 = (f32[4,600,128]{2,1,0:T(8,128)}, f32[608,128]{1,0:T(8,128)}, f32[64,128]{1,0:T(8,128)}, f32[64,128]{1,0:T(8,128)}) custom-call(f32[2]{0:T(128)} %occ_ref.1, s32[1,128]{1,0:T(1,128)} %bitcast.1, f32[2,2,160,128]{3,2,1,0:T(8,128)} %wave_hbm.3, bf16[512,960]{1,0:T(8,128)(2,1)} %constant.12.clone.ztab_hbm, ...), custom_call_target="tpu_custom_call" | custom-call | flops 10000000000 | bytes 8000000 | tf_op jit(solution)/shard_map/pallas_call | solution.py:765
  30.0 7.6 %shard_map.167.sums_ref = f32[64,128]{1,0:T(8,128)} custom-call(s32[96]{0:T(128)} %place_ref.3, s32[96]{0:T(128)} %atom_ref.3, f32[4,600,128]{2,1,0:T(8,128)} %get-tuple-element.9.psi_ref, f32[96,64,128]{2,1,0:T(8,128)} %proj_hbm.3), custom_call_target="tpu_custom_call" | custom-call | flops 1000000000 | bytes 8000000 | tf_op jit(solution)/shard_map/pallas_call | solution.py:773
  37.7 0.4 collective-permute-start.1
  38.0 1.4 %collective-permute-start = (f32[64,128]{1,0:T(8,128)}, f32[64,128]{1,0:T(8,128)S(1)}, u32[]{:S(2)}, u32[]{:S(2)}) collective-permute-start(f32[64,128]{1,0:T(8,128)} %shard_map.167.sums_ref), channel_id=1, source_target_pairs={{0,1},{1,2},{2,3},{3,4},{4,5},{5,6},{6,7},{7,8},{8,9},{9,10},{10,1... | collective-permute-start | bytes 98312 | tf_op jit(solution)/shard_map/ppermute | solution.py:776
  39.5 1.8 %collective-permute-done.1.after_ref = f32[64,128]{1,0:T(8,128)S(1)} collective-permute-done((f32[64,128]{1,0:T(8,128)}, f32[64,128]{1,0:T(8,128)S(1)}, u32[]{:S(2)}, u32[]{:S(2)}) %collective-permute-start.1) | collective-permute-done | bytes 32800 | tf_op jit(solution)/shard_map/ppermute | solution.py:777
  41.3 0.0 copy-start
  41.3 0.0 collective-permute-done.before_ref
  41.3 0.6 copy-done
  41.9 0.0 copy-start.1
  41.9 0.6 copy-done.1
  42.5 7.1 %shard_map.168.h_ref = f32[4,600,128]{2,1,0:T(8,128)} custom-call(s32[96]{0:T(128)} %place_ref.3, s32[96]{0:T(128)} %atom_ref.3, f32[64,128]{1,0:T(8,128)} %shard_map.167.sums_ref, f32[64,128]{1,0:T(8,128)} %copy-done.1, f32[64,128]{1,0:T(8,128)} %copy-done, f32[64,64]{1,0:T(8,128)} %coupling_ref.1, f32[4,600,128]{2,1,0:T(8,128)} %get-tuple-element.9.psi_ref, ...), custom_call_target="tpu_custom_call" | custom-call | flops 1000000000 | bytes 8000000 | tf_op jit(solution)/shard_map/pallas_call | solution.py:778
  49.6 40.2 %shard_map.169 = (f32[2,2,160,128]{3,2,1,0:T(8,128)}, f32[3,25600]{1,0:T(4,128)}, f32[3,25600]{1,0:T(4,128)}) custom-call(f32[64,128]{1,0:T(8,128)} %get-tuple-element.7.xs_ref, f32[64,128]{1,0:T(8,128)} %get-tuple-element.8.ys_ref, s32[1,128]{1,0:T(1,128)} %bitcast.2, f32[4,600,128]{2,1,0:T(8,128)} %shard_map.168.h_ref, ...), custom_call_target="tpu_custom_call" | custom-call | flops 10000000000 | bytes 8000000 | tf_op jit(solution)/shard_map/pallas_call | solution.py:781
  89.9 1.7 %copy.21 = f32[2,2,160,128]{3,2,1,0:T(8,128)} copy(f32[2,2,160,128]{3,2,1,0:T(8,128)} %get-tuple-element.14) | data formatting | bytes 655360
  91.6 1.8 %copy.22 = f32[3,25600]{1,0:T(4,128)} copy(f32[3,25600]{1,0:T(4,128)} %get-tuple-element.15) | data formatting | bytes 614400
  93.4 1.8 %copy.23 = f32[3,25600]{1,0:T(4,128)} copy(f32[3,25600]{1,0:T(4,128)} %get-tuple-element.16) | data formatting | bytes 614400
Async XLA Ops:
  37.7 3.6 %collective-permute-start.1 = (f32[64,128]{1,0:T(8,128)}, f32[64,128]{1,0:T(8,128)S(1)}, u32[]{:S(2)}, u32[]{:S(2)}) collective-permute-start(f32[64,128]{1,0:T(8,128)} %shard_map.167.sums_ref), channel_id=1, source_target_pairs={{1,0},{2,1},{3,2},{4,3},{5,4},{6,5},{7,6},{8,7},{9,8},{10,9},{11,1... | collective-permute-start | bytes 98312 | tf_op jit(solution)/shard_map/ppermute | solution.py:777
  38.0 3.3 %collective-permute-start = (f32[64,128]{1,0:T(8,128)}, f32[64,128]{1,0:T(8,128)S(1)}, u32[]{:S(2)}, u32[]{:S(2)}) collective-permute-start(f32[64,128]{1,0:T(8,128)} %shard_map.167.sums_ref), channel_id=1, source_target_pairs={{0,1},{1,2},{2,3},{3,4},{4,5},{5,6},{6,7},{7,8},{8,9},{9,10},{10,1... | collective-permute-start | bytes 98312 | tf_op jit(solution)/shard_map/ppermute | solution.py:776
  41.3 0.6 copy-start
  41.9 0.6 copy-start.1

commit v2 on v0

v2 whole, which is shorter than its diff:
```python
import math

import jax
import jax.numpy as jnp
import numpy as np
from jax import lax
from jax.experimental import pallas as pl
from jax.experimental.pallas import tpu as pltpu
from jax.sharding import PartitionSpec as P

N = 160
ZP = 3
N_FFT = 64
NBLK = 96
ATOM_DEV = 16
ATOMS = 1024
BANDS_AXIS = 4
SLICE = 152
SHIFT = 52
BOX = 104
HALF = 56
F32 = jnp.float32
BF16 = jnp.bfloat16

lda_factor = (3.0 / math.pi) ** (1.0 / 3.0)


def parts(table):
    high = table.astype(np.float32).astype(jnp.bfloat16)
    low = (table - high.astype(np.float64)).astype(np.float32).astype(jnp.bfloat16)
    return high, low


def real_form(cosine, sine):
    return np.block([[cosine, -sine], [sine, cosine]])


def z_tables():
    slot, place = np.meshgrid(np.arange(8), np.arange(N_FFT), indexing="ij")
    out = np.zeros((N_FFT, 8, 2, N))
    g = np.arange(N)
    for f in range(N_FFT):
        for s in range(ZP):
            z = s * N_FFT + f
            if z < N:
                phase = 2 * np.pi / N * ((z * g) % N)
                c, d = np.cos(phase) / math.sqrt(N), np.sin(phase) / math.sqrt(N)
                out[f, s, 0], out[f, s, 1] = c, -d
                out[f, 3 + s, 0], out[f, 3 + s, 1] = d, c
    forward = out.reshape(N_FFT * 8, 2 * N)
    return forward, forward.T


def x_tables():
    rows = np.array([4 * k + g for g in range(4) for k in range(40)])
    compact = np.array([2 * h + p for p in range(2) for h in range(HALF)])
    phase = 2 * np.pi / N * ((rows[:, None] * (compact[None, :] - SHIFT)) % N)
    keep = (compact < BOX)[None, :] / math.sqrt(N)
    ahead = real_form(np.cos(phase) * keep, np.sin(phase) * keep)
    phase = phase.T
    keep = keep.T
    back = real_form(np.cos(phase) * keep, -np.sin(phase) * keep)
    return ahead, back


PAIRS = tuple((j, g) for g in range(4) for j in (g, g + 1))


def y_tables():
    compact = np.arange(128)
    out = []
    for j, g in PAIRS:
        flat = 128 * j + np.arange(128)
        keep = ((flat // N == g)[None, :] & (compact < BOX)[:, None]) / math.sqrt(N)
        phase = 2 * np.pi / N * (((compact[:, None] - SHIFT) * (flat % N)[None, :]) % N)
        c, d = np.cos(phase) * keep, np.sin(phase) * keep
        out.append(np.block([[c, d], [-d, c]]))
    return np.stack(out)


def stack3(table, axis):
    high, low = parts(table)
    return np.concatenate([high, low, high], axis=axis)


def make_tables():
    z_ahead, z_back = z_tables()
    x_ahead, x_back = x_tables()
    y_ahead = y_tables()
    y_back = np.swapaxes(y_ahead, 1, 2)
    return dict(
        z_ahead=stack3(z_ahead, 1),
        z_back=stack3(z_back, 1),
        x_ahead=stack3(x_ahead, 1),
        x_back=stack3(x_back, 1),
        y_ahead=np.stack(parts(y_ahead), axis=1),
        y_back=np.stack(parts(y_back), axis=1),
    )


def split(value):
    high = value.astype(BF16)
    return high, (value - high.astype(F32)).astype(BF16)


def dot(left, right):
    return lax.dot_general(left, right, (((1,), (0,)), ((), ())), preferred_element_type=F32)


def dot_nt(left, right):
    return lax.dot_general(left, right, (((1,), (1,)), ((), ())), preferred_element_type=F32)


def lhs3(value):
    high, low = split(value)
    return jnp.concatenate([high, high, low], axis=1)


def rhs3(value):
    high, low = split(value)
    return jnp.concatenate([high, high, low], axis=0)


def grid_xy(stick_ref):
    column = stick_ref[...].astype(F32)
    x = jnp.floor((column + 0.5) * (1.0 / N))
    y = column - N * x
    return x, y


def block_row(place):
    slot = (place >= 200).astype(jnp.int32) + (place >= 400).astype(jnp.int32)
    inside = place - 200 * slot
    fifth = (inside * 6554) >> 15
    return slot * 200 + (inside - 5 * fifth) * 40 + fifth


ROWS = [(b, o, s) for b in range(2) for o in range(2) for s in range(ZP)]
CHUNK = 4
PART = 12 * HALF


def ahead_of(me, step):
    return lax.rem(me + step, N_FFT)


def behind(me, step):
    return lax.rem(me + N_FFT - step, N_FFT)


def fft_copy(source, target, send_sem, recv_sem, device):
    return pltpu.make_async_remote_copy(
        src_ref=source,
        dst_ref=target,
        send_sem=send_sem,
        recv_sem=recv_sem,
        device_id={"fft": device},
        device_id_type=pl.DeviceIdType.MESH,
    )


def band_copy(source, target, send_sem, recv_sem, device):
    return pltpu.make_async_remote_copy(
        src_ref=source,
        dst_ref=target,
        send_sem=send_sem,
        recv_sem=recv_sem,
        device_id={"band": device},
        device_id_type=pl.DeviceIdType.MESH,
    )


def put(send_ref, land_ref, send_sems, recv_sems, me, step):
    target = ahead_of(me, step)
    return fft_copy(
        send_ref.at[target], land_ref.at[me], send_sems.at[step], recv_sems.at[step], target
    )


def landing(send_ref, land_ref, send_sems, recv_sems, me, step):
    source = behind(me, step)
    return fft_copy(
        send_ref.at[source], land_ref.at[source], send_sems.at[step], recv_sems.at[step], source
    )


def whole(
    occ_ref,
    place_ref,
    atom_ref,
    place_row_ref,
    atom_row_ref,
    stick_ref,
    coupling_ref,
    potential_ref,
    wave_hbm,
    ztab_hbm,
    xtab_hbm,
    ytab_hbm,
    proj_hbm,
    xback_hbm,
    yback_hbm,
    land_ref,
    full_ref,
    wave_ref,
    ztab_ref,
    xtab_ref,
    ytab_ref,
    proj_ref,
    xback_ref,
    yback_ref,
    send_ref,
    first_ref,
    last_ref,
    grid_ref,
    mid_ref,
    psi_ref,
    power_ref,
    piece_ref,
    sums_ref,
    before_ref,
    after_ref,
    weight_ref,
    pot_ref,
    add_ref,
    h_ref,
    left_ref,
    part_ref,
    mine_ref,
    total_ref,
    sems,
    send_sems,
    recv_sems,
    send2_sems,
    recv2_sems,
    halo_send_sems,
    halo_recv_sems,
    band_send_sems,
    band_recv_sems,
):
    me = lax.axis_index("fft")
    group = lax.axis_index("band")
    barrier = pltpu.get_barrier_semaphore()
    loads = [
        pltpu.make_async_copy(source, target, sems.at[i])
        for i, (source, target) in enumerate(
            [
                (wave_hbm, wave_ref),
                (ztab_hbm, ztab_ref),
                (xtab_hbm, xtab_ref),
                (ytab_hbm, ytab_ref),
                (proj_hbm, proj_ref),
                (xback_hbm, xback_ref),
                (yback_hbm, yback_ref),
            ]
        )
    ]
    for load in loads:
        load.start()

    def greet(step, carry):
        pl.semaphore_signal(
            barrier,
            inc=1,
            device_id={"fft": ahead_of(me, step)},
            device_id_type=pl.DeviceIdType.MESH,
        )
        return carry

    lax.fori_loop(1, N_FFT, greet, 0, unroll=3)
    for step in range(1, 4):
        pl.semaphore_signal(
            barrier,
            inc=1,
            device_id={"band": lax.rem(group + step, 4)},
            device_id_type=pl.DeviceIdType.MESH,
        )

    grid_ref[...] = jnp.zeros_like(grid_ref)
    x, y = grid_xy(stick_ref)
    half = N // 2
    xc = jnp.where(x < half, x, x - N) + SHIFT
    yc = jnp.where(y < half, y, y - N) + SHIFT
    loads[0].wait()
    loads[1].wait()
    both = [jnp.concatenate([wave_ref[0, b], wave_ref[1, b]], axis=0) for b in range(2)]
    result = dot(ztab_ref[...], rhs3(jnp.concatenate(both, axis=1)))
    for b in range(2):
        send_ref[:, 8 * b : 8 * b + 8, :] = result[:, 128 * b : 128 * b + 128].reshape(
            N_FFT, 8, 128
        )
    send_ref[:, 6:7, :] = jnp.broadcast_to(xc[None], (N_FFT, 1, 128))
    send_ref[:, 7:8, :] = jnp.broadcast_to(yc[None], (N_FFT, 1, 128))

    pl.semaphore_wait(barrier, N_FFT - 1 + 3)

    def send(step, carry):
        put(send_ref, first_ref, send_sems, recv_sems, me, step).start()
        return carry

    lax.fori_loop(1, N_FFT, send, 0, unroll=3)
    first_ref[me] = send_ref[me]

    row_id = lax.broadcasted_iota(jnp.int32, (HALF, 128), 0).astype(F32)
    lane_id = lax.broadcasted_iota(jnp.int32, (256, 128), 0).astype(F32)

    def scatter(chunk, carry):
        lefts, rights = [], []
        for i in range(CHUNK):
            step = chunk * CHUNK + i

            @pl.when(step > 0)
            def _():
                landing(send_ref, first_ref, send_sems, recv_sems, me, step).wait_recv()

            tile = first_ref[behind(me, step)]
            x, y = tile[6:7], tile[7:8]
            x2 = jnp.floor(x * 0.5)
            here = row_id == x2
            rights.append((lane_id == (x - 2.0 * x2) * 128.0 + y).astype(F32).astype(BF16))
            high = tile.astype(BF16).astype(F32)
            picked = [
                jnp.where(here, piece[8 * b + 3 * o + s : 8 * b + 3 * o + s + 1], 0.0)
                for piece in (high, tile - high)
                for b, o, s in ROWS
            ]
            lefts.append(jnp.concatenate(picked, axis=0).astype(BF16))
        grid_ref[...] += dot_nt(jnp.concatenate(lefts, axis=1), jnp.concatenate(rights, axis=1))
        return carry

    lax.fori_loop(0, N_FFT // CHUNK, scatter, 0)

    columns = []
    for b in range(2):
        for s in range(ZP):
            rows = []
            for o in range(2):
                first = (b * 6 + o * 3 + s) * HALF
                for parity in range(2):
                    lanes = slice(128 * parity, 128 * parity + 128)
                    rows.append(
                        grid_ref[first : first + HALF, lanes]
                        + grid_ref[PART + first : PART + first + HALF, lanes]
                    )
            columns.append(jnp.concatenate(rows, axis=0))
    loads[2].wait()
    mixed = dot(xtab_ref[...], rhs3(jnp.concatenate(columns, axis=1)))
    for g in range(4):
        for o in range(2):
            first = (o * 4 + g) * 40
            for bs in range(6):
                mid_ref[g, 40 * bs : 40 * bs + 40, 128 * o : 128 * o + 128] = mixed[
                    first : first + 40, 128 * bs : 128 * bs + 128
                ]
    lefts = [lhs3(mid_ref[g]) for g in range(4)]
    loads[3].wait()
    for j in range(5):
        total = None
        for at, (tile, g) in enumerate(PAIRS):
            if tile == j:
                high, low = ytab_ref[at, 0], ytab_ref[at, 1]
                term = dot(lefts[g], jnp.concatenate([high, low, high], axis=0))
                total = term if total is None else total + term
        for b in range(2):
            for s in range(ZP):
                bs = b * ZP + s
                for o in range(2):
                    first = s * 200 + j * 40
                    psi_ref[b * 2 + o, first : first + 40, :] = total[
                        40 * bs : 40 * bs + 40, 128 * o : 128 * o + 128
                    ]

    def power(b):
        re, im = psi_ref[2 * b], psi_ref[2 * b + 1]
        return re * re + im * im

    power_ref[:600] = occ_ref[0] * power(0) + occ_ref[1] * power(1)
    power_ref[600:] = jnp.zeros((4 * SLICE - 600, 128), F32)

    def rows_of(index):
        return pl.ds(pl.multiple_of(index * SLICE, 8), SLICE)

    def quarter(step):
        target = lax.rem(group + step, 4)
        return band_copy(
            power_ref.at[rows_of(target)],
            part_ref.at[step - 1],
            band_send_sems.at[step - 1],
            band_recv_sems.at[step - 1],
            target,
        )

    for step in range(1, 4):
        quarter(step).start()

    def fetch(k, carry):
        row = block_row(place_ref[k])
        for c in range(4):
            piece_ref[pl.ds(4 * k + c, 1), :] = psi_ref[c, pl.ds(row, 1), :]
        return carry

    lax.fori_loop(0, NBLK, fetch, 0, unroll=4)
    loads[4].wait()
    lane = lax.broadcasted_iota(jnp.int32, (64, 128), 1)
    picks = []
    for part in range(3):
        piece_high, piece_low = split(piece_ref[128 * part : 128 * part + 128])
        piece_both = jnp.concatenate([piece_high, piece_high], axis=1)
        found = jnp.zeros((64, 128), F32)
        for chunk in range(2):
            first = part * 32 + chunk * 16
            high, low = split(proj_ref[first : first + 16].reshape(1024, 128))
            values = dot_nt(jnp.concatenate([high, low], axis=1), piece_both)
            values = values + dot_nt(high, piece_low)
            for m in range(16):
                own = lax.div(lane, 4) == chunk * 16 + m
                found = jnp.where(own, values[64 * m : 64 * m + 64], found)
        picks.append(found)
    found = jnp.concatenate(picks, axis=1)
    base = me * ATOM_DEV - ATOM_DEV // 2
    near = lax.rem(atom_row_ref[...] - base + 2 * ATOMS, ATOMS).astype(F32)
    spread = lax.div(lax.broadcasted_iota(jnp.int32, (NBLK, 4 * NBLK), 1), 4)
    spread = spread == lax.broadcasted_iota(jnp.int32, (NBLK, 4 * NBLK), 0)
    near = dot(
        jnp.broadcast_to(near, (16, NBLK)).astype(BF16), spread.astype(F32).astype(BF16)
    )[0:1]
    column = lax.broadcasted_iota(jnp.int32, (128, 4 * NBLK), 0)
    owner = lax.rem(lax.broadcasted_iota(jnp.int32, (128, 4 * NBLK), 1), 4).astype(F32) + 4.0 * near
    member = (owner == column.astype(F32)).astype(F32).astype(BF16)
    high, low = split(found)
    sums_ref[...] = dot_nt(
        jnp.concatenate([high, low], axis=1), jnp.concatenate([member, member], axis=1)
    )
    after_me, before_me = ahead_of(me, 1), behind(me, 1)
    to_after = fft_copy(
        sums_ref, before_ref, halo_send_sems.at[0], halo_recv_sems.at[0], after_me
    )
    to_before = fft_copy(
        sums_ref, after_ref, halo_send_sems.at[1], halo_recv_sems.at[1], before_me
    )
    to_after.start()
    to_before.start()

    for q in range(200):
        row = (q % 5) * 40 + q // 5
        pot_ref[:, row, :] = potential_ref[:, 128 * q : 128 * q + 128]

    for step in range(1, 4):
        quarter(step).wait()
    mine_ref[...] = power_ref[rows_of(group)] + part_ref[0] + part_ref[1] + part_ref[2]
    total_ref[rows_of(group)] = mine_ref[...]

    def share(step):
        return band_copy(
            mine_ref,
            total_ref.at[rows_of(group)],
            band_send_sems.at[2 + step],
            band_recv_sems.at[2 + step],
            lax.rem(group + step, 4),
        )

    for step in range(1, 4):
        share(step).start()

    to_after.wait()
    to_before.wait()
    beside = jnp.where(
        lane < 64, pltpu.roll(before_ref[...], 64, 1), pltpu.roll(after_ref[...], 64, 1)
    )
    weight = lax.dot_general(
        coupling_ref[...],
        sums_ref[...] + beside,
        (((1,), (0,)), ((), ())),
        precision=lax.Precision.HIGHEST,
        preferred_element_type=F32,
    )
    for n in range(128):
        weight_ref[n] = jnp.broadcast_to(weight[:, n : n + 1], (64, 128))

    def added(k, carry):
        first = ((atom_ref[k] - base) & (2 * ATOM_DEV - 1)) * 4
        values = proj_ref[k]
        for c in range(4):
            add_ref[c, pl.ds(k, 1), :] = jnp.sum(
                values * weight_ref[first + c], axis=0, keepdims=True
            )
        return carry

    lax.fori_loop(0, NBLK, added, 0, unroll=2)
    place = place_row_ref[...]
    slot = (place >= 200).astype(jnp.int32) + (place >= 400).astype(jnp.int32)
    inside = place - 200 * slot
    fifth = (inside * 6554) >> 15
    place = slot * 200 + (inside - 5 * fifth) * 40 + fifth
    block_id = lax.broadcasted_iota(jnp.int32, (600, NBLK), 0)
    spot = (block_id == place).astype(F32).astype(BF16)
    potential = pot_ref[...].reshape(600, 128)
    for c in range(4):
        high, low = split(add_ref[c])
        h_ref[c] = potential * psi_ref[c] + (dot(spot, high) + dot(spot, low))

    lefts = []
    for j in range(5):
        rows = []
        for b in range(2):
            for s in range(ZP):
                first = s * 200 + j * 40
                rows.append(
                    jnp.concatenate(
                        [h_ref[b * 2 + o, first : first + 40, :] for o in range(2)], axis=1
                    )
                )
        lefts.append(lhs3(jnp.concatenate(rows, axis=0)))
    loads[6].wait()
    turned = []
    for g in range(4):
        total = None
        for at, (j, owner) in enumerate(PAIRS):
            if owner == g:
                high, low = yback_ref[at, 0], yback_ref[at, 1]
                term = dot(lefts[j], jnp.concatenate([high, low, high], axis=0))
                total = term if total is None else total + term
        turned.append(total)
    columns = []
    for bs in range(6):
        rows = []
        for o in range(2):
            for g in range(4):
                rows.append(turned[g][40 * bs : 40 * bs + 40, 128 * o : 128 * o + 128])
        columns.append(jnp.concatenate(rows, axis=0))
    loads[5].wait()
    spectrum = dot(xback_ref[...], rhs3(jnp.concatenate(columns, axis=1)))
    for at, (b, o, s) in enumerate(ROWS):
        bs = b * ZP + s
        for parity in range(2):
            first = (o * 2 + parity) * HALF
            grid_ref[at * HALF : at * HALF + HALF, 128 * parity : 128 * parity + 128] = spectrum[
                first : first + HALF, 128 * bs : 128 * bs + 128
            ]
    high, low = split(grid_ref[:PART])
    left_ref[:PART] = high
    left_ref[PART:] = low

    id256 = lax.broadcasted_iota(jnp.int32, (256, 256), 0).astype(F32)
    zeros = jnp.zeros((2, 256), F32)

    def gather(pair, carry):
        steps = (2 * pair, 2 * pair + 1)
        targets = [ahead_of(me, step) for step in steps]
        tiles = [first_ref[target, 0:8, :] for target in targets]
        x = jnp.concatenate([tile[6:7] for tile in tiles], axis=1)
        y = jnp.concatenate([tile[7:8] for tile in tiles], axis=1)
        x2 = jnp.floor(x * 0.5)
        here = id256[:HALF] == x2
        spot = (id256 == (x - 2.0 * x2) * 128.0 + y).astype(F32).astype(BF16)
        values = dot(left_ref[...], spot)
        rows = []
        for at in range(12):
            first = at * HALF
            one = values[first : first + HALF] + values[PART + first : PART + first + HALF]
            rows.append(jnp.sum(jnp.where(here, one, 0.0), axis=0, keepdims=True))
            if at % 6 == 5:
                rows.append(zeros)
        result = jnp.concatenate(rows, axis=0)
        for i in range(2):
            send2_ref[targets[i]] = result[:, 128 * i : 128 * i + 128]

        @pl.when(pair > 0)
        def _():
            put(send2_ref, last_ref, send2_sems, recv2_sems, me, steps[0]).start()

        put(send2_ref, last_ref, send2_sems, recv2_sems, me, steps[1]).start()
        return carry

    def sent(step, carry):
        put(send_ref, first_ref, send_sems, recv_sems, me, step).wait_send()
        return carry

    lax.fori_loop(1, N_FFT, sent, 0, unroll=3)
    send2_ref = send_ref
    lax.fori_loop(0, N_FFT // 2, gather, 0)
    last_ref[me] = send2_ref[me]

    for step in range(1, 4):
        source = lax.rem(group + 4 - step, 4)
        band_copy(
            mine_ref,
            total_ref.at[rows_of(source)],
            band_send_sems.at[2 + step],
            band_recv_sems.at[2 + step],
            source,
        ).wait_recv()
    for step in range(1, 4):
        share(step).wait_send()
    full_ref[...] = total_ref[...]

    def arrive(step, carry):
        landing(send2_ref, last_ref, send2_sems, recv2_sems, me, step).wait_recv()
        return carry

    lax.fori_loop(1, N_FFT, arrive, 0, unroll=3)
    land_ref[...] = last_ref[...]

    def sent2(step, carry):
        put(send2_ref, last_ref, send2_sems, recv2_sems, me, step).wait_send()
        return carry

    lax.fori_loop(1, N_FFT, sent2, 0, unroll=3)


def finish(
    stick_ref,
    land_ref,
    full_ref,
    core_ref,
    wave_ref,
    ztab_ref,
    out_ref,
    dens_ref,
    field_ref,
    box_ref,
    core3_ref,
):
    me = lax.axis_index("fft")
    for q in range(200):
        row = (q % 5) * 40 + q // 5
        core3_ref[:, row, :] = core_ref[:, 128 * q : 128 * q + 128]
    density = full_ref[:600].reshape(ZP, 200, 128)
    box_ref[...] = density
    for q in range(200):
        row = (q % 5) * 40 + q // 5
        dens_ref[:, 128 * q : 128 * q + 128] = box_ref[:, row, :]
    slot = lax.broadcasted_iota(jnp.int32, (ZP, 200, 128), 0)
    field = -lda_factor * jnp.exp(jnp.log(density + core3_ref[...]) * (1.0 / 3.0))
    core3_ref[...] = jnp.where(slot * N_FFT + me < N, field, 0.0)
    for q in range(200):
        row = (q % 5) * 40 + q // 5
        field_ref[:, 128 * q : 128 * q + 128] = core3_ref[:, row, :]
    x, y = grid_xy(stick_ref)
    half = N // 2
    x = jnp.where(x < half, x, x - N) / N
    y = jnp.where(y < half, y, y - N) / N
    g = lax.broadcasted_iota(jnp.int32, (N, 128), 0)
    z = jnp.where(g < half, g, g - N).astype(F32) / N
    kinetic = 2.0 * (x * x + y * y) + 2.0 * (z * z)
    both = [land_ref[:, 8 * b : 8 * b + 8, :].reshape(N_FFT * 8, 128) for b in range(2)]
    result = dot(ztab_ref[...], rhs3(jnp.concatenate(both, axis=1)))
    for o in range(2):
        for b in range(2):
            spectrum = result[N * o : N * o + N, 128 * b : 128 * b + 128]
            out_ref[o, b] = spectrum + kinetic * wave_ref[o, b]


VMEM = pltpu.VMEM
DMA = pltpu.SemaphoreType.DMA
SMEM_SPEC = pl.BlockSpec(memory_space=pltpu.SMEM)
VMEM_SPEC = pl.BlockSpec(memory_space=pltpu.VMEM)
ANY_SPEC = pl.BlockSpec(memory_space=pl.ANY)
LIMIT = 56 * 1024 * 1024


def call(body, in_specs, outs, scratch=(), flops=0, size=0, remote=None):
    options = {} if remote is None else dict(collective_id=remote, has_side_effects=True)
    return pl.pallas_call(
        body,
        out_shape=outs,
        in_specs=in_specs,
        out_specs=jax.tree.map(lambda _: VMEM_SPEC, outs),
        scratch_shapes=list(scratch),
        compiler_params=pltpu.CompilerParams(vmem_limit_bytes=LIMIT, **options),
        cost_estimate=pl.CostEstimate(flops=flops, bytes_accessed=size, transcendentals=0),
    )


def shape(*dims):
    return jax.ShapeDtypeStruct(dims, F32)


def make_calls():
    ytab = VMEM((8, 2, 256, 256), BF16)
    tiles = VMEM((N_FFT, 16, 128), F32)
    block = VMEM((64, 128), F32)
    big = call(
        whole,
        [SMEM_SPEC] * 3 + [VMEM_SPEC] * 5 + [ANY_SPEC] * 7,
        (shape(N_FFT, 16, 128), shape(4 * SLICE, 128)),
        (
            VMEM((2, 2, N, 128), F32),
            VMEM((8 * N_FFT, 6 * N), BF16),
            VMEM((2 * N, 12 * HALF), BF16),
            ytab,
            VMEM((NBLK, 64, 128), F32),
            VMEM((4 * HALF, 6 * N), BF16),
            ytab,
            tiles,
            tiles,
            tiles,
            VMEM((2 * PART, 256), F32),
            VMEM((4, 240, 256), F32),
            VMEM((4, 600, 128), F32),
            VMEM((4 * SLICE, 128), F32),
            VMEM((4 * NBLK, 128), F32),
            block,
            block,
            block,
            VMEM((128, 64, 128), F32),
            VMEM((ZP, 200, 128), F32),
            VMEM((4, NBLK, 128), F32),
            VMEM((4, 600, 128), F32),
            VMEM((2 * PART, 256), BF16),
            VMEM((3, SLICE, 128), F32),
            VMEM((SLICE, 128), F32),
            VMEM((4 * SLICE, 128), F32),
            DMA((7,)),
            DMA((N_FFT,)),
            DMA((N_FFT,)),
            DMA((N_FFT,)),
            DMA((N_FFT,)),
            DMA((2,)),
            DMA((2,)),
            DMA((6,)),
            DMA((6,)),
        ),
        20_000_000_000,
        16_000_000,
        0,
    )
    last = call(
        finish,
        [VMEM_SPEC] * 6,
        (shape(2, 2, N, 128), shape(ZP, N * N), shape(ZP, N * N)),
        (VMEM((ZP, 200, 128), F32), VMEM((ZP, 200, 128), F32)),
        500_000_000,
        4_000_000,
    )
    return big, last


def local(
    tables,
    wave_coef,
    stick_map,
    local_potential,
    core_density,
    occupations,
    block_place,
    block_atom,
    projectors,
    coupling,
):
    big, last = make_calls()
    stick_row = stick_map.reshape(1, 128)
    land, full = big(
        occupations,
        block_place,
        block_atom,
        block_place.reshape(1, NBLK),
        block_atom.reshape(1, NBLK),
        stick_row,
        coupling,
        local_potential,
        wave_coef,
        tables["z_ahead"],
        tables["x_ahead"],
        tables["y_ahead"],
        projectors,
        tables["x_back"],
        tables["y_back"],
    )
    return last(stick_row, land, full, core_density, wave_coef, tables["z_back"])


def solution(mesh):
    tables = {name: jnp.asarray(value) for name, value in make_tables().items()}

    def run(*args):
        return local(tables, *args)

    return jax.shard_map(
        run,
        mesh=mesh,
        in_specs=(
            P(None, "band", None, "fft"),
            P("fft"),
            P("fft", None),
            P("fft", None),
            P("band"),
            P("fft"),
            P("fft"),
            P("fft", None, None),
            P(),
        ),
        out_specs=(P(None, "band", None, "fft"), P("fft", None), P("fft", None)),
        check_vma=False,
    )
```

time: 120 us -> 67.1 us (0.56)
  waiting for transfers between devices: 35.3 us -> 0 us
  Pallas kernels: 42 us -> 66.3 us
  starting transfers between devices: 23 us -> 0 us
  between operations: 14.1 us -> 0.64 us
  local copies, waits for them, and re-layouts: 2.95 us -> 0 us
  other arithmetic: 2.5 us -> 0 us
    pallas_call x4 -> x2, Pallas kernels: 42 us -> 66.3 us  [the longest x1 62.7 us: local(): big(occupations, block_place, block_atom, block_place.reshape(1, NBLK), b...]
    all_to_all x2 -> x0, starting transfers between devices: 22.1 us -> none  [the longest x1 11.8 us: local(): lax.all_to_all(result, 'fft', split_axis=0, concat_axis=0, tiled=True)]
    psum x1 -> x0, waiting for transfers between devices: 19.4 us -> none  [local(): density = lax.psum(group_density, 'band')]
    all_to_all x2 -> x0, waiting for transfers between devices: 12.4 us -> none  [the longest x1 12.4 us: local(): lax.all_to_all(sent, 'fft', split_axis=0, concat_axis=0, tiled=True)]
    ppermute x2 -> x0, waiting for transfers between devices: 3.51 us -> none  [the longest x1 2.21 us: local(): after = lax.ppermute(sums, 'fft', down)]
    unnamed x13 -> x0, local copies, waits for them, and re-layouts: 2.95 us -> none
    mul x2 -> x0, other arithmetic: 2.5 us -> none  [local(): -lda_factor * jnp.cbrt(density + core_density) * valid[:, None]]
  transfers between devices with their start and end apart: 5 -> 0, of which waited for: 4 -> 0; matrix products, arithmetic and copies ran while one was open for 2% -> 0% of each run, Pallas kernels for 17% -> 0%
where the time goes in v2:
time: 67.1 us; the launch traced here: 67 us
  Pallas kernels  66.3 us (99%)
    pallas_call x1, Pallas kernels, local(): big(occupations, block_place, block_atom, block_place.reshape(1, NBLK), b...  62.7 us
    pallas_call x1, Pallas kernels, local(): last(stick_row, land, full, core_density, wave_coef, tables['z_back'])  3.6 us

profile of v2, /device:TPU:1, one launch (start us, length us, event | category | flops | bytes accessed | tf_op | source)
XLA Modules:
  0.0 67.0 jit_solution(6515881178024276241)
XLA Ops:
  0.6 62.7 %shard_map.166 = (f32[64,16,128]{2,1,0:T(8,128)}, f32[608,128]{1,0:T(8,128)}) custom-call(f32[2]{0:T(128)} %occ_ref.1, s32[96]{0:T(128)} %place_ref.1, s32[96]{0:T(128)} %atom_ref.1, s32[1,96]{1,0:T(1,128)} %bitcast.5, s32[1,96]{1,0:T(1,128)} %bitcast.6, s32[1,128]{1,0:T(1,128)} %bitcast.3, f32[64,64]{1,0:T(8,128)} %coupling_ref.1, ...), custom_call_target="tpu_custom_call" | custom-call | flops 20000000000 | bytes 16000000 | tf_op jit(solution)/shard_map/pallas_call | solution.py:753
  63.4 3.6 %shard_map.167 = (f32[2,2,160,128]{3,2,1,0:T(8,128)}, f32[3,25600]{1,0:T(4,128)}, f32[3,25600]{1,0:T(4,128)}) custom-call(s32[1,128]{1,0:T(1,128)} %bitcast.4, f32[64,16,128]{2,1,0:T(8,128)} %get-tuple-element.5.land_ref, f32[608,128]{1,0:T(8,128)} %get-tuple-element.6.full_ref, f32[3,25600]{1,0:T(4,128)} %core_ref.1, f32[2,2,160,128]{3,2,1,0:T(8,128)} %wave_ref.1, ...), custom_call_target="tpu_custom_call" | custom-call | flops 500000000 | bytes 4000000 | tf_op jit(solution)/shard_map/pallas_call | solution.py:770

commit v3 on v2

--- a/solution.py
+++ b/solution.py
@@ -137,6 +137,8 @@
 
 ROWS = [(b, o, s) for b in range(2) for o in range(2) for s in range(ZP)]
 CHUNK = 4
+UNROLL_S = 4
+UNROLL_G = 8
 PART = 12 * HALF
 
 
@@ -170,18 +172,26 @@
     )
 
 
-def put(send_ref, land_ref, send_sems, recv_sems, me, step):
+def put(send_ref, land_ref, send_sem, recv_sem, me, step):
     target = ahead_of(me, step)
-    return fft_copy(
-        send_ref.at[target], land_ref.at[me], send_sems.at[step], recv_sems.at[step], target
-    )
-
-
-def landing(send_ref, land_ref, send_sems, recv_sems, me, step):
-    source = behind(me, step)
-    return fft_copy(
-        send_ref.at[source], land_ref.at[source], send_sems.at[step], recv_sems.at[step], source
-    )
+    return fft_copy(send_ref.at[target], land_ref.at[me], send_sem, recv_sem, target)
+
+
+def bytes_of(ref, count, sem):
+    return pltpu.make_async_copy(ref.at[pl.ds(0, count)], ref.at[pl.ds(0, count)], sem)
+
+
+def in_groups(body, count, group):
+    for i in range(group):
+        body(i)
+
+    def one(at, carry):
+        for i in range(group):
+            body(at * group + i)
+        return carry
+
+    if count > group:
+        lax.fori_loop(1, count // group, one, 0)
 
 
 def whole(
@@ -231,8 +241,6 @@
     sems,
     send_sems,
     recv_sems,
-    send2_sems,
-    recv2_sems,
     halo_send_sems,
     halo_recv_sems,
     band_send_sems,
@@ -295,7 +303,8 @@
     pl.semaphore_wait(barrier, N_FFT - 1 + 3)
 
     def send(step, carry):
-        put(send_ref, first_ref, send_sems, recv_sems, me, step).start()
+        chunk = lax.div(step, CHUNK)
+        put(send_ref, first_ref, send_sems.at[0], recv_sems.at[chunk], me, step).start()
         return carry
 
     lax.fori_loop(1, N_FFT, send, 0, unroll=3)
@@ -304,15 +313,12 @@
     row_id = lax.broadcasted_iota(jnp.int32, (HALF, 128), 0).astype(F32)
     lane_id = lax.broadcasted_iota(jnp.int32, (256, 128), 0).astype(F32)
 
-    def scatter(chunk, carry):
+    def scatter(chunk):
+        own = 1 if isinstance(chunk, int) and chunk == 0 else 0
+        bytes_of(first_ref, CHUNK - own, recv_sems.at[chunk]).wait()
         lefts, rights = [], []
         for i in range(CHUNK):
             step = chunk * CHUNK + i
-
-            @pl.when(step > 0)
-            def _():
-                landing(send_ref, first_ref, send_sems, recv_sems, me, step).wait_recv()
-
             tile = first_ref[behind(me, step)]
             x, y = tile[6:7], tile[7:8]
             x2 = jnp.floor(x * 0.5)
@@ -326,9 +332,8 @@
             ]
             lefts.append(jnp.concatenate(picked, axis=0).astype(BF16))
         grid_ref[...] += dot_nt(jnp.concatenate(lefts, axis=1), jnp.concatenate(rights, axis=1))
-        return carry
-
-    lax.fori_loop(0, N_FFT // CHUNK, scatter, 0)
+
+    in_groups(scatter, N_FFT // CHUNK, UNROLL_S)
 
     columns = []
     for b in range(2):
@@ -544,7 +549,7 @@
     id256 = lax.broadcasted_iota(jnp.int32, (256, 256), 0).astype(F32)
     zeros = jnp.zeros((2, 256), F32)
 
-    def gather(pair, carry):
+    def gather(pair):
         steps = (2 * pair, 2 * pair + 1)
         targets = [ahead_of(me, step) for step in steps]
         tiles = [first_ref[target, 0:8, :] for target in targets]
@@ -565,20 +570,13 @@
         for i in range(2):
             send2_ref[targets[i]] = result[:, 128 * i : 128 * i + 128]
 
-        @pl.when(pair > 0)
-        def _():
-            put(send2_ref, last_ref, send2_sems, recv2_sems, me, steps[0]).start()
-
-        put(send2_ref, last_ref, send2_sems, recv2_sems, me, steps[1]).start()
-        return carry
-
-    def sent(step, carry):
-        put(send_ref, first_ref, send_sems, recv_sems, me, step).wait_send()
-        return carry
-
-    lax.fori_loop(1, N_FFT, sent, 0, unroll=3)
+        for step in steps:
+            if not isinstance(step, int) or step > 0:
+                put(send2_ref, last_ref, send_sems.at[1], send_sems.at[2], me, step).start()
+
+    bytes_of(send_ref, N_FFT - 1, send_sems.at[0]).wait()
     send2_ref = send_ref
-    lax.fori_loop(0, N_FFT // 2, gather, 0)
+    in_groups(gather, N_FFT // 2, UNROLL_G)
     last_ref[me] = send2_ref[me]
 
     for step in range(1, 4):
@@ -594,18 +592,9 @@
         share(step).wait_send()
     full_ref[...] = total_ref[...]
 
-    def arrive(step, carry):
-        landing(send2_ref, last_ref, send2_sems, recv2_sems, me, step).wait_recv()
-        return carry
-
-    lax.fori_loop(1, N_FFT, arrive, 0, unroll=3)
+    bytes_of(last_ref, N_FFT - 1, send_sems.at[2]).wait()
     land_ref[...] = last_ref[...]
-
-    def sent2(step, carry):
-        put(send2_ref, last_ref, send2_sems, recv2_sems, me, step).wait_send()
-        return carry
-
-    lax.fori_loop(1, N_FFT, sent2, 0, unroll=3)
+    bytes_of(send2_ref, N_FFT - 1, send_sems.at[1]).wait()
 
 
 def finish(
@@ -712,10 +701,8 @@
             VMEM((SLICE, 128), F32),
             VMEM((4 * SLICE, 128), F32),
             DMA((7,)),
-            DMA((N_FFT,)),
-            DMA((N_FFT,)),
-            DMA((N_FFT,)),
-            DMA((N_FFT,)),
+            DMA((3,)),
+            DMA((N_FFT // CHUNK,)),
             DMA((2,)),
             DMA((2,)),
             DMA((6,)),

time: 67.1 us -> 72.9 us (1.086)
  Pallas kernels: 66.3 us -> 71.9 us
    pallas_call x1, Pallas kernels: 62.7 us -> 68.3 us  [local(): big(occupations, block_place, block_atom, block_place.reshape(1, NBLK), b...]
where the time goes in v3:
time: 72.9 us; the launch traced here: 72.6 us
  Pallas kernels  71.9 us (99%)
    pallas_call x1, Pallas kernels, local(): big(occupations, block_place, block_atom, block_place.reshape(1, NBLK), b...  68.3 us
    pallas_call x1, Pallas kernels, local(): last(stick_row, land, full, core_density, wave_coef, tables['z_back'])  3.6 us

profile of v3, /device:TPU:1, one launch (start us, length us, event | category | flops | bytes accessed | tf_op | source)
XLA Modules:
  0.0 72.6 jit_solution(1037886139413103793)
XLA Ops:
  0.6 68.3 %shard_map.166 = (f32[64,16,128]{2,1,0:T(8,128)}, f32[608,128]{1,0:T(8,128)}) custom-call(f32[2]{0:T(128)} %occ_ref.1, s32[96]{0:T(128)} %place_ref.1, s32[96]{0:T(128)} %atom_ref.1, s32[1,96]{1,0:T(1,128)} %bitcast.5, s32[1,96]{1,0:T(1,128)} %bitcast.6, s32[1,128]{1,0:T(1,128)} %bitcast.3, f32[64,64]{1,0:T(8,128)} %coupling_ref.1, ...), custom_call_target="tpu_custom_call" | custom-call | flops 20000000000 | bytes 16000000 | tf_op jit(solution)/shard_map/pallas_call | solution.py:740
  69.0 3.6 %shard_map.167 = (f32[2,2,160,128]{3,2,1,0:T(8,128)}, f32[3,25600]{1,0:T(4,128)}, f32[3,25600]{1,0:T(4,128)}) custom-call(s32[1,128]{1,0:T(1,128)} %bitcast.4, f32[64,16,128]{2,1,0:T(8,128)} %get-tuple-element.5.land_ref, f32[608,128]{1,0:T(8,128)} %get-tuple-element.6.full_ref, f32[3,25600]{1,0:T(4,128)} %core_ref.1, f32[2,2,160,128]{3,2,1,0:T(8,128)} %wave_ref.1, ...), custom_call_target="tpu_custom_call" | custom-call | flops 500000000 | bytes 4000000 | tf_op jit(solution)/shard_map/pallas_call | solution.py:757

commit v4 on v3

--- a/solution.py
+++ b/solution.py
@@ -137,8 +137,8 @@
 
 ROWS = [(b, o, s) for b in range(2) for o in range(2) for s in range(ZP)]
 CHUNK = 4
-UNROLL_S = 4
-UNROLL_G = 8
+UNROLL_S = 2
+UNROLL_G = 4
 PART = 12 * HALF
 
 
@@ -179,19 +179,6 @@
 
 def bytes_of(ref, count, sem):
     return pltpu.make_async_copy(ref.at[pl.ds(0, count)], ref.at[pl.ds(0, count)], sem)
-
-
-def in_groups(body, count, group):
-    for i in range(group):
-        body(i)
-
-    def one(at, carry):
-        for i in range(group):
-            body(at * group + i)
-        return carry
-
-    if count > group:
-        lax.fori_loop(1, count // group, one, 0)
 
 
 def whole(
@@ -308,14 +295,12 @@
         return carry
 
     lax.fori_loop(1, N_FFT, send, 0, unroll=3)
-    first_ref[me] = send_ref[me]
+    pltpu.make_async_copy(send_ref.at[me], first_ref.at[me], recv_sems.at[0]).start()
 
     row_id = lax.broadcasted_iota(jnp.int32, (HALF, 128), 0).astype(F32)
     lane_id = lax.broadcasted_iota(jnp.int32, (256, 128), 0).astype(F32)
 
     def scatter(chunk):
-        own = 1 if isinstance(chunk, int) and chunk == 0 else 0
-        bytes_of(first_ref, CHUNK - own, recv_sems.at[chunk]).wait()
         lefts, rights = [], []
         for i in range(CHUNK):
             step = chunk * CHUNK + i
@@ -333,7 +318,14 @@
             lefts.append(jnp.concatenate(picked, axis=0).astype(BF16))
         grid_ref[...] += dot_nt(jnp.concatenate(lefts, axis=1), jnp.concatenate(rights, axis=1))
 
-    in_groups(scatter, N_FFT // CHUNK, UNROLL_S)
+    def scatter_group(at, carry):
+        for i in range(UNROLL_S):
+            bytes_of(first_ref, CHUNK, recv_sems.at[at * UNROLL_S + i]).wait()
+        for i in range(UNROLL_S):
+            scatter(at * UNROLL_S + i)
+        return carry
+
+    lax.fori_loop(0, N_FFT // CHUNK // UNROLL_S, scatter_group, 0)
 
     columns = []
     for b in range(2):
@@ -570,14 +562,26 @@
         for i in range(2):
             send2_ref[targets[i]] = result[:, 128 * i : 128 * i + 128]
 
-        for step in steps:
-            if not isinstance(step, int) or step > 0:
-                put(send2_ref, last_ref, send_sems.at[1], send_sems.at[2], me, step).start()
 
     bytes_of(send_ref, N_FFT - 1, send_sems.at[0]).wait()
     send2_ref = send_ref
-    in_groups(gather, N_FFT // 2, UNROLL_G)
-    last_ref[me] = send2_ref[me]
+
+    def gather_group(at, carry):
+        for i in range(UNROLL_G):
+            gather(at * UNROLL_G + i)
+        first = at * (2 * UNROLL_G)
+        for i in range(1, 2 * UNROLL_G):
+            put(send2_ref, last_ref, send_sems.at[1], send_sems.at[2], me, first + i).start()
+
+        @pl.when(at > 0)
+        def _():
+            put(send2_ref, last_ref, send_sems.at[1], send_sems.at[2], me, first).start()
+
+        return carry
+
+    lax.fori_loop(0, N_FFT // 2 // UNROLL_G, gather_group, 0)
+    own = pltpu.make_async_copy(send2_ref.at[me], last_ref.at[me], send_sems.at[2])
+    own.start()
 
     for step in range(1, 4):
         source = lax.rem(group + 4 - step, 4)
@@ -592,7 +596,7 @@
         share(step).wait_send()
     full_ref[...] = total_ref[...]
 
-    bytes_of(last_ref, N_FFT - 1, send_sems.at[2]).wait()
+    bytes_of(last_ref, N_FFT, send_sems.at[2]).wait()
     land_ref[...] = last_ref[...]
     bytes_of(send2_ref, N_FFT - 1, send_sems.at[1]).wait()
 

time: 72.9 us -> 60.5 us (0.83)
  Pallas kernels: 71.9 us -> 59.7 us
    pallas_call x1, Pallas kernels: 68.3 us -> 56.1 us  [local(): big(occupations, block_place, block_atom, block_place.reshape(1, NBLK), b...]
where the time goes in v4:
time: 60.5 us; the launch traced here: 60.3 us
  Pallas kernels  59.7 us (99%)
  between operations  0.64 us (1%)
    pallas_call x1, Pallas kernels, local(): big(occupations, block_place, block_atom, block_place.reshape(1, NBLK), b...  56.1 us
    pallas_call x1, Pallas kernels, local(): last(stick_row, land, full, core_density, wave_coef, tables['z_back'])  3.6 us

profile of v4, /device:TPU:1, one launch (start us, length us, event | category | flops | bytes accessed | tf_op | source)
XLA Modules:
  0.0 60.3 jit_solution(7059854279897866347)
XLA Ops:
  0.6 56.1 %shard_map.166 = (f32[64,16,128]{2,1,0:T(8,128)}, f32[608,128]{1,0:T(8,128)}) custom-call(f32[2]{0:T(128)} %occ_ref.1, s32[96]{0:T(128)} %place_ref.1, s32[96]{0:T(128)} %atom_ref.1, s32[1,96]{1,0:T(1,128)} %bitcast.5, s32[1,96]{1,0:T(1,128)} %bitcast.6, s32[1,128]{1,0:T(1,128)} %bitcast.3, f32[64,64]{1,0:T(8,128)} %coupling_ref.1, ...), custom_call_target="tpu_custom_call" | custom-call | flops 20000000000 | bytes 16000000 | tf_op jit(solution)/shard_map/pallas_call | solution.py:744
  56.8 3.6 %shard_map.167 = (f32[2,2,160,128]{3,2,1,0:T(8,128)}, f32[3,25600]{1,0:T(4,128)}, f32[3,25600]{1,0:T(4,128)}) custom-call(s32[1,128]{1,0:T(1,128)} %bitcast.4, f32[64,16,128]{2,1,0:T(8,128)} %get-tuple-element.5.land_ref, f32[608,128]{1,0:T(8,128)} %get-tuple-element.6.full_ref, f32[3,25600]{1,0:T(4,128)} %core_ref.1, f32[2,2,160,128]{3,2,1,0:T(8,128)} %wave_ref.1, ...), custom_call_target="tpu_custom_call" | custom-call | flops 500000000 | bytes 4000000 | tf_op jit(solution)/shard_map/pallas_call | solution.py:761

commit v5 on v4

--- a/solution.py
+++ b/solution.py
@@ -137,7 +137,7 @@
 
 ROWS = [(b, o, s) for b in range(2) for o in range(2) for s in range(ZP)]
 CHUNK = 4
-UNROLL_S = 2
+UNROLL_S = 4
 UNROLL_G = 4
 PART = 12 * HALF
 
@@ -396,7 +396,7 @@
             piece_ref[pl.ds(4 * k + c, 1), :] = psi_ref[c, pl.ds(row, 1), :]
         return carry
 
-    lax.fori_loop(0, NBLK, fetch, 0, unroll=4)
+    lax.fori_loop(0, NBLK, fetch, 0, unroll=2)
     loads[4].wait()
     lane = lax.broadcasted_iota(jnp.int32, (64, 128), 1)
     picks = []

time: 60.5 us -> 60 us (level)
  no operation moved by 1% of the time
where the time goes in v5:
time: 60 us; the launch traced here: 59.8 us
  Pallas kernels  59.2 us (99%)
  between operations  0.64 us (1%)
    pallas_call x1, Pallas kernels, local(): big(occupations, block_place, block_atom, block_place.reshape(1, NBLK), b...  55.6 us
    pallas_call x1, Pallas kernels, local(): last(stick_row, land, full, core_density, wave_coef, tables['z_back'])  3.6 us

profile of v5, /device:TPU:1, one launch (start us, length us, event | category | flops | bytes accessed | tf_op | source)
XLA Modules:
  0.0 59.8 jit_solution(8665384543275528763)
XLA Ops:
  0.6 55.6 %shard_map.166 = (f32[64,16,128]{2,1,0:T(8,128)}, f32[608,128]{1,0:T(8,128)}) custom-call(f32[2]{0:T(128)} %occ_ref.1, s32[96]{0:T(128)} %place_ref.1, s32[96]{0:T(128)} %atom_ref.1, s32[1,96]{1,0:T(1,128)} %bitcast.5, s32[1,96]{1,0:T(1,128)} %bitcast.6, s32[1,128]{1,0:T(1,128)} %bitcast.3, f32[64,64]{1,0:T(8,128)} %coupling_ref.1, ...), custom_call_target="tpu_custom_call" | custom-call | flops 20000000000 | bytes 16000000 | tf_op jit(solution)/shard_map/pallas_call | solution.py:744
  56.2 3.6 %shard_map.167 = (f32[2,2,160,128]{3,2,1,0:T(8,128)}, f32[3,25600]{1,0:T(4,128)}, f32[3,25600]{1,0:T(4,128)}) custom-call(s32[1,128]{1,0:T(1,128)} %bitcast.4, f32[64,16,128]{2,1,0:T(8,128)} %get-tuple-element.5.land_ref, f32[608,128]{1,0:T(8,128)} %get-tuple-element.6.full_ref, f32[3,25600]{1,0:T(4,128)} %core_ref.1, f32[2,2,160,128]{3,2,1,0:T(8,128)} %wave_ref.1, ...), custom_call_target="tpu_custom_call" | custom-call | flops 500000000 | bytes 4000000 | tf_op jit(solution)/shard_map/pallas_call | solution.py:761
